TPU v7x, 256 devices: a whole 4x4x8 slice. The times are simulated.
256 devices in a mesh: lon: 16 (over y, x), lat: 8 (over z), depth: 2 (over core).
Axes of the slice: x: 4, y: 4, z: 8, core: 2. Of those that a mesh axis runs over, the one named last changes fastest.
Arguments:
- states: float32 [4, 20, 256, 4096], P(None, 'depth', 'lat', 'lon'), may hold values from -2.5 to 2.5
- direction: float32 [20, 256, 4096], P('depth', 'lat', 'lon'), may hold values from -6 to 6
- mixing: float32 [20, 256, 4096], P('depth', 'lat', 'lon'), may hold values from 0.3 to 1
- level_dz: float32 [20], P('depth'), may hold values from 0.5 to 2
- lat_width: float32 [256], P('lat'), may hold values from 0.5 to 2
- cost_weight: float32 [20, 256], P(None, 'lat'), may hold values from 0.1 to 1
- ocean_columns: int32 [256, 4096], P('lat', 'lon'), may hold values 0 or 1
- atlantic: int32 [256, 4096], P('lat', 'lon'), may hold values 0 or 1
- levels: int32 [256, 4096], P('lat', 'lon'), may hold values from 4 to 20
Outputs:
- hessian_product: float32 [20, 256, 4096], P('depth', 'lat', 'lon')
- gradient: float32 [20, 256, 4096], P('depth', 'lat', 'lon')
- overturning: float32 [20, 256], P('depth', 'lat')
All inputs are finite; a program needn't handle non-finite values. No bound on the sum of `ocean_columns` or of `atlantic` on one device may be relied on, other than what follows from the above.
Results may differ from a plain program's by a relative error of at most 0.00002.
Values sent between devices are 32-bit elements; how exact they have to be, the bound alone decides.
A program may use at most 64 MiB of HBM per device.

v0:
```python
import math

import jax
import jax.numpy as jnp
from jax import lax
from jax.sharding import PartitionSpec as P

diffusion_step = 0.08
cubic_drag = 0.15


def extended(block, sides, width):
    for axis, dim in sides:
        count = lax.axis_size(axis)
        forward = [(i, i + 1) for i in range(count - 1)]
        backward = [(target, source) for source, target in forward]
        low = lax.ppermute(
            lax.slice_in_dim(block, block.shape[dim] - width, None, axis=dim), axis, forward
        )
        high = lax.ppermute(lax.slice_in_dim(block, 0, width, axis=dim), axis, backward)
        block = jnp.concatenate([low, block, high], axis=dim)
    return block


def carried_in(part, axis, combine, identity, reverse):
    count = lax.axis_size(axis)
    place = lax.axis_index(axis)
    ahead = count - 1 - place if reverse else place
    gathered = lax.all_gather(part, axis)
    state = jnp.zeros_like(part) + jnp.asarray(identity, part.dtype)

    def one(lap, state):
        source = count - 1 - lap if reverse else lap
        return combine(state, lax.dynamic_index_in_dim(gathered, source, 0, False))

    return lax.fori_loop(0, ahead, one, state)


def neighbours(field_pad, couple_pad):
    centre = field_pad[1:-1, 1:-1, 1:-1]
    summed = jnp.zeros_like(centre)
    for which in range(3):
        for offset in (0, 2):
            window = [slice(1, -1), slice(1, -1), slice(1, -1)]
            window[which] = slice(offset, offset + centre.shape[which])
            window = tuple(window)
            summed = summed + couple_pad[window] * (field_pad[window] - centre)
    return couple_pad[1:-1, 1:-1, 1:-1] * summed


def add_terms(earlier, later):
    return earlier + later


def shards(
    states, direction, mixing, level_dz, lat_width, cost_weight, ocean_columns, atlantic, levels
):
    sections = states.shape[0]
    layers, rows, columns = direction.shape
    start = lax.axis_index("depth") * layers
    full_lon = columns * lax.axis_size("lon")
    full_depth = layers * lax.axis_size("depth")
    level_index = start + lax.broadcasted_iota(jnp.int32, (layers, 1, 1), 0)
    wetness = (ocean_columns[None] * (level_index < levels[None]).astype(jnp.int32)).astype(
        jnp.float32
    )
    coupling = mixing * wetness
    area = (
        atlantic.astype(jnp.float32)[None]
        * level_dz[:, None, None]
        * lat_width[None, :, None]
        * (1.0 / math.sqrt(full_lon * full_depth))
    )
    last = states[sections - 1]
    first = extended(
        jnp.stack([direction, coupling, last]), (("lon", 3), ("lat", 2), ("depth", 1)), 1
    )
    couple_pad = first[1]
    last_pad = first[2]
    tangent = direction
    tangent_pad = first[0]
    tangents = []
    for number in range(sections):
        tangents.append(tangent)
        saved = states[number]
        tangent = wetness * (
            tangent
            + diffusion_step * neighbours(tangent_pad, couple_pad)
            - 3.0 * cubic_drag * saved * saved * tangent
        )
        if number + 1 < sections:
            tangent_pad = extended(tangent, (("lon", 2), ("lat", 1), ("depth", 0)), 1)
    final = wetness * (
        last + diffusion_step * neighbours(last_pad, couple_pad) - cubic_drag * last * last * last
    )
    zonal = jnp.stack([jnp.sum(area * final, axis=2), jnp.sum(area * tangent, axis=2)])
    grid_scale = math.sqrt(full_lon)
    zonal_all = lax.psum(zonal, "lon")
    local_suffix = jnp.flip(jnp.cumsum(jnp.flip(zonal_all, 1), axis=1), 1)
    deeper = carried_in(
        local_suffix[:, 0], "depth", add_terms, jnp.zeros((2, rows), jnp.float32), True
    )
    stream = local_suffix + deeper[:, None, :]
    own_weight = lax.dynamic_slice_in_dim(cost_weight, start, layers, 0)
    forcing = own_weight[None] * stream * grid_scale
    local_prefix = jnp.cumsum(forcing, axis=1)
    shallower = carried_in(
        local_prefix[:, -1], "depth", add_terms, jnp.zeros((2, rows), jnp.float32), False
    )
    prefix = local_prefix + shallower[:, None, :]
    lam = area * prefix[0][:, :, None]
    tan_adj = area * prefix[1][:, :, None]
    for number in reversed(range(sections)):
        padded = extended(jnp.stack([tan_adj, lam]), (("lon", 3), ("lat", 2), ("depth", 1)), 1)
        saved = states[number]
        damping = 3.0 * cubic_drag * saved * saved
        new_adj = (
            wetness
            * (tan_adj + diffusion_step * neighbours(padded[0], couple_pad) - damping * tan_adj)
            - 6.0 * cubic_drag * wetness * saved * tangents[number] * lam
        )
        lam = wetness * (lam + diffusion_step * neighbours(padded[1], couple_pad) - damping * lam)
        tan_adj = new_adj
    return (tan_adj, lam, stream[0])


def solution(mesh):
    placed = (
        P(None, "depth", "lat", "lon"),
        P("depth", "lat", "lon"),
        P("depth", "lat", "lon"),
        P("depth"),
        P("lat"),
        P(None, "lat"),
        P("lat", "lon"),
        P("lat", "lon"),
        P("lat", "lon"),
    )
    return jax.shard_map(
        shards,
        mesh=mesh,
        in_specs=placed,
        out_specs=(P("depth", "lat", "lon"), P("depth", "lat", "lon"), P("depth", "lat")),
        check_vma=False,
    )
```

profile of v0, /device:TPU:1, one launch (start us, length us, event | category | flops | bytes accessed | tf_op | source)
XLA Modules:
  0.0 334.5 jit_solution(4205973883993179158)
XLA Ops:
  3.1 4.0 %collective-permute-start = (f32[3,10,32,1]{3,2,1,0:T(8,128)S(1)}, f32[3,10,32,1]{3,2,1,0:T(8,128)S(1)}, u32[]{:S(2)}, u32[]{:S(2)}) collective-permute-start(f32[3,10,32,1]{3,2,1,0:T(8,128)S(1)} %get-tuple-element.133), channel_id=1, source_target_pairs={{0,16},{16,32},{32,48},{48,64},{64,80},{80,96},{96,112},{112,128},... | collective-permute-start | bytes 11528 | tf_op jit(solution)/shard_map/ppermute | solution.py:17
  8.4 8.5 %collective-permute-done = f32[3,10,32,1]{3,2,1,0:T(8,128)S(1)} collective-permute-done((f32[3,10,32,1]{3,2,1,0:T(8,128)S(1)}, f32[3,10,32,1]{3,2,1,0:T(8,128)S(1)}, u32[]{:S(2)}, u32[]{:S(2)}) %collective-permute-start) | collective-permute-done | bytes 3872 | tf_op jit(solution)/shard_map/ppermute | solution.py:17
  17.0 3.8 %collective-permute-done.1 = f32[3,10,32,1]{3,2,1,0:T(8,128)S(1)} collective-permute-done((f32[3,10,32,1]{3,2,1,0:T(8,128)S(1)}, f32[3,10,32,1]{3,2,1,0:T(8,128)S(1)}, u32[]{:S(2)}, u32[]{:S(2)}) %collective-permute-start.1) | collective-permute-done | bytes 3872 | tf_op jit(solution)/shard_map/ppermute | solution.py:20
  26.0 3.7 %collective-permute-done.3 = f32[3,10,1,258]{3,2,1,0:T(1,128)S(1)} collective-permute-done((f32[3,10,1,258]{3,2,1,0:T(1,128)S(1)}, f32[3,10,1,258]{3,2,1,0:T(1,128)S(1)}, u32[]{:S(2)}, u32[]{:S(2)}) %collective-permute-start.3) | collective-permute-done | bytes 30992 | tf_op jit(solution)/shard_map/ppermute | solution.py:20
  31.1 5.0 %collective-permute-start.5 = (f32[3,1,34,258]{3,2,1,0:T(8,128)S(1)}, f32[3,1,34,258]{3,2,1,0:T(8,128)S(1)}, u32[]{:S(2)}, u32[]{:S(2)}) collective-permute-start(f32[3,1,34,258]{3,2,1,0:T(8,128)S(1)} %get-tuple-element.106), channel_id=1, source_target_pairs={{1,0},{3,2},{5,4},{7,6},{9,8},{11,10},{13,12},{15,14},{17,16},{19,... | collective-permute-start | bytes 315800 | tf_op jit(solution)/shard_map/ppermute | solution.py:20
  46.8 3.8 %collective-permute-done.7 = f32[10,32,1]{2,1,0:T(8,128)S(1)} collective-permute-done((f32[10,32,1]{2,1,0:T(8,128)S(1)}, f32[10,32,1]{2,1,0:T(8,128)S(1)}, u32[]{:S(2)}, u32[]{:S(2)}) %collective-permute-start.7) | collective-permute-done | bytes 1312 | tf_op jit(solution)/shard_map/ppermute | solution.py:20
  50.8 3.5 %collective-permute-start.8 = (f32[10,1,258]{2,1,0:T(1,128)S(1)}, f32[10,1,258]{2,1,0:T(1,128)S(1)}, u32[]{:S(2)}, u32[]{:S(2)}) collective-permute-start(f32[10,1,258]{2,1,0:T(1,128)S(1)} %get-tuple-element.153), channel_id=1, source_target_pairs={{0,2},{2,4},{4,6},{6,8},{8,10},{10,12},{12,14},{1,3},{3,5},{5,7},{... | collective-permute-start | bytes 30968 | tf_op jit(solution)/shard_map/ppermute | solution.py:17
  55.6 4.5 %collective-permute-done.9 = f32[10,1,258]{2,1,0:T(1,128)S(1)} collective-permute-done((f32[10,1,258]{2,1,0:T(1,128)S(1)}, f32[10,1,258]{2,1,0:T(1,128)S(1)}, u32[]{:S(2)}, u32[]{:S(2)}) %collective-permute-start.9) | collective-permute-done | bytes 10352 | tf_op jit(solution)/shard_map/ppermute | solution.py:20
  61.5 4.6 %collective-permute-start.11 = (f32[1,34,258]{2,1,0:T(8,128)S(1)}, f32[1,34,258]{2,1,0:T(8,128)S(1)}, u32[]{:S(2)}, u32[]{:S(2)}) collective-permute-start(f32[1,34,258]{2,1,0:T(8,128)S(1)} %get-tuple-element.140), channel_id=1, source_target_pairs={{1,0},{3,2},{5,4},{7,6},{9,8},{11,10},{13,12},{15,14},{17,16},{19,... | collective-permute-start | bytes 105272 | tf_op jit(solution)/shard_map/ppermute | solution.py:20
  68.2 4.7 %collective-permute-start.12 = (f32[10,32,1]{2,1,0:T(8,128)S(1)}, f32[10,32,1]{2,1,0:T(8,128)S(1)}, u32[]{:S(2)}, u32[]{:S(2)}) collective-permute-start(f32[10,32,1]{2,1,0:T(8,128)S(1)} %get-tuple-element.157), channel_id=1, source_target_pairs={{0,16},{16,32},{32,48},{48,64},{64,80},{80,96},{96,112},{112,128},... | collective-permute-start | bytes 3848 | tf_op jit(solution)/shard_map/ppermute | solution.py:17
  76.1 3.8 %collective-permute-done.13 = f32[10,32,1]{2,1,0:T(8,128)S(1)} collective-permute-done((f32[10,32,1]{2,1,0:T(8,128)S(1)}, f32[10,32,1]{2,1,0:T(8,128)S(1)}, u32[]{:S(2)}, u32[]{:S(2)}) %collective-permute-start.13) | collective-permute-done | bytes 1312 | tf_op jit(solution)/shard_map/ppermute | solution.py:20
  80.0 4.8 %collective-permute-start.14 = (f32[10,1,258]{2,1,0:T(1,128)S(1)}, f32[10,1,258]{2,1,0:T(1,128)S(1)}, u32[]{:S(2)}, u32[]{:S(2)}) collective-permute-start(f32[10,1,258]{2,1,0:T(1,128)S(1)} %get-tuple-element.151), channel_id=1, source_target_pairs={{0,2},{2,4},{4,6},{6,8},{8,10},{10,12},{12,14},{1,3},{3,5},{5,7},{... | collective-permute-start | bytes 30968 | tf_op jit(solution)/shard_map/ppermute | solution.py:17
  91.1 4.6 %collective-permute-start.17 = (f32[1,34,258]{2,1,0:T(8,128)S(1)}, f32[1,34,258]{2,1,0:T(8,128)S(1)}, u32[]{:S(2)}, u32[]{:S(2)}) collective-permute-start(f32[1,34,258]{2,1,0:T(8,128)S(1)} %get-tuple-element.138), channel_id=1, source_target_pairs={{1,0},{3,2},{5,4},{7,6},{9,8},{11,10},{13,12},{15,14},{17,16},{19,... | collective-permute-start | bytes 105272 | tf_op jit(solution)/shard_map/ppermute | solution.py:20
  99.1 4.7 %collective-permute-start.18 = (f32[10,32,1]{2,1,0:T(8,128)}, f32[10,32,1]{2,1,0:T(8,128)}, u32[]{:S(2)}, u32[]{:S(2)}) collective-permute-start(f32[10,32,1]{2,1,0:T(8,128)} %get-tuple-element.155), channel_id=1, source_target_pairs={{0,16},{16,32},{32,48},{48,64},{64,80},{80,96},{96,112},{112,128},... | collective-permute-start | bytes 3848 | tf_op jit(solution)/shard_map/ppermute | solution.py:17
  106.7 4.4 %collective-permute-done.19 = f32[10,32,1]{2,1,0:T(8,128)} collective-permute-done((f32[10,32,1]{2,1,0:T(8,128)}, f32[10,32,1]{2,1,0:T(8,128)}, u32[]{:S(2)}, u32[]{:S(2)}) %collective-permute-start.19) | collective-permute-done | bytes 1312 | tf_op jit(solution)/shard_map/ppermute | solution.py:20
  112.8 4.2 %collective-permute-start.20 = (f32[10,1,258]{2,1,0:T(1,128)}, f32[10,1,258]{2,1,0:T(1,128)}, u32[]{:S(2)}, u32[]{:S(2)}) collective-permute-start(f32[10,1,258]{2,1,0:T(1,128)} %get-tuple-element.149), channel_id=1, source_target_pairs={{0,2},{2,4},{4,6},{6,8},{8,10},{10,12},{12,14},{1,3},{3,5},{5,7},{... | collective-permute-start | bytes 30968 | tf_op jit(solution)/shard_map/ppermute | solution.py:17
  124.1 4.8 %collective-permute-start.23 = (f32[1,34,258]{2,1,0:T(8,128)S(1)}, f32[1,34,258]{2,1,0:T(8,128)S(1)}, u32[]{:S(2)}, u32[]{:S(2)}) collective-permute-start(f32[1,34,258]{2,1,0:T(8,128)S(1)} %get-tuple-element.136), channel_id=1, source_target_pairs={{1,0},{3,2},{5,4},{7,6},{9,8},{11,10},{13,12},{15,14},{17,16},{19,... | collective-permute-start | bytes 105272 | tf_op jit(solution)/shard_map/ppermute | solution.py:20
  133.7 57.3 %psum.7 = f32[2,10,32]{2,1,0:T(8,128)S(1)} all-reduce(f32[2,10,32]{2,1,0:T(8,128)S(1)} %rev.7), channel_id=1, replica_groups=mesh['lon'=16,'lat'=8,'depth'=2] {'lon'}, use_global_device_ids=true, to_apply=%region_2.0 | all-reduce | flops 640 | bytes 5120 | tf_op jit(solution)/shard_map/psum | solution.py:98
  191.0 14.7 %all-gather = f32[4,1,32]{2,1,0:T(1,128)S(1)} all-gather(f32[2,1,32]{2,1,0:T(1,128)S(1)} %slice.792), channel_id=2, replica_groups=mesh['lon'=16,'lat'=8,'depth'=2] {'depth'}, dimensions={0}, use_global_device_ids=true | all-gather | bytes 768 | tf_op jit(solution)/shard_map/all_gather | solution.py:29
  210.6 5.8 %collective-permute-done.24 = f32[2,10,32,1]{3,2,1,0:T(8,128)S(1)} collective-permute-done((f32[2,10,32,1]{3,2,1,0:T(8,128)S(1)}, f32[2,10,32,1]{3,2,1,0:T(8,128)S(1)}, u32[]{:S(2)}, u32[]{:S(2)}) %collective-permute-start.24) | collective-permute-done | bytes 2592 | tf_op jit(solution)/shard_map/ppermute | solution.py:17
  216.4 3.8 %collective-permute-done.25 = f32[2,10,32,1]{3,2,1,0:T(8,128)S(1)} collective-permute-done((f32[2,10,32,1]{3,2,1,0:T(8,128)S(1)}, f32[2,10,32,1]{3,2,1,0:T(8,128)S(1)}, u32[]{:S(2)}, u32[]{:S(2)}) %collective-permute-start.25) | collective-permute-done | bytes 2592 | tf_op jit(solution)/shard_map/ppermute | solution.py:20
  228.8 4.5 %collective-permute-start.29 = (f32[2,1,34,258]{3,2,1,0:T(8,128)S(1)}, f32[2,1,34,258]{3,2,1,0:T(8,128)S(1)}, u32[]{:S(2)}, u32[]{:S(2)}) collective-permute-start(f32[2,1,34,258]{3,2,1,0:T(8,128)S(1)} %get-tuple-element.124), channel_id=1, source_target_pairs={{1,0},{3,2},{5,4},{7,6},{9,8},{11,10},{13,12},{15,14},{17,16},{19,... | collective-permute-start | bytes 210536 | tf_op jit(solution)/shard_map/ppermute | solution.py:20
  240.9 5.5 %collective-permute-done.30 = f32[2,10,32,1]{3,2,1,0:T(8,128)S(1)} collective-permute-done((f32[2,10,32,1]{3,2,1,0:T(8,128)S(1)}, f32[2,10,32,1]{3,2,1,0:T(8,128)S(1)}, u32[]{:S(2)}, u32[]{:S(2)}) %collective-permute-start.30) | collective-permute-done | bytes 2592 | tf_op jit(solution)/shard_map/ppermute | solution.py:17
  246.5 3.8 %collective-permute-done.31 = f32[2,10,32,1]{3,2,1,0:T(8,128)S(1)} collective-permute-done((f32[2,10,32,1]{3,2,1,0:T(8,128)S(1)}, f32[2,10,32,1]{3,2,1,0:T(8,128)S(1)}, u32[]{:S(2)}, u32[]{:S(2)}) %collective-permute-start.31) | collective-permute-done | bytes 2592 | tf_op jit(solution)/shard_map/ppermute | solution.py:20
  259.5 4.7 %collective-permute-start.35 = (f32[2,1,34,258]{3,2,1,0:T(8,128)S(1)}, f32[2,1,34,258]{3,2,1,0:T(8,128)S(1)}, u32[]{:S(2)}, u32[]{:S(2)}) collective-permute-start(f32[2,1,34,258]{3,2,1,0:T(8,128)S(1)} %get-tuple-element.122), channel_id=1, source_target_pairs={{1,0},{3,2},{5,4},{7,6},{9,8},{11,10},{13,12},{15,14},{17,16},{19,... | collective-permute-start | bytes 210536 | tf_op jit(solution)/shard_map/ppermute | solution.py:20
  272.6 5.4 %collective-permute-done.36 = f32[2,10,32,1]{3,2,1,0:T(8,128)S(1)} collective-permute-done((f32[2,10,32,1]{3,2,1,0:T(8,128)S(1)}, f32[2,10,32,1]{3,2,1,0:T(8,128)S(1)}, u32[]{:S(2)}, u32[]{:S(2)}) %collective-permute-start.36) | collective-permute-done | bytes 2592 | tf_op jit(solution)/shard_map/ppermute | solution.py:17
  278.0 3.8 %collective-permute-done.37 = f32[2,10,32,1]{3,2,1,0:T(8,128)S(1)} collective-permute-done((f32[2,10,32,1]{3,2,1,0:T(8,128)S(1)}, f32[2,10,32,1]{3,2,1,0:T(8,128)S(1)}, u32[]{:S(2)}, u32[]{:S(2)}) %collective-permute-start.37) | collective-permute-done | bytes 2592 | tf_op jit(solution)/shard_map/ppermute | solution.py:20
  291.0 4.9 %collective-permute-start.41 = (f32[2,1,34,258]{3,2,1,0:T(8,128)S(1)}, f32[2,1,34,258]{3,2,1,0:T(8,128)S(1)}, u32[]{:S(2)}, u32[]{:S(2)}) collective-permute-start(f32[2,1,34,258]{3,2,1,0:T(8,128)S(1)} %get-tuple-element.120), channel_id=1, source_target_pairs={{1,0},{3,2},{5,4},{7,6},{9,8},{11,10},{13,12},{15,14},{17,16},{19,... | collective-permute-start | bytes 210536 | tf_op jit(solution)/shard_map/ppermute | solution.py:20
  299.9 4.0 %collective-permute-start.42 = (f32[2,10,32,1]{3,2,1,0:T(8,128)S(1)}, f32[2,10,32,1]{3,2,1,0:T(8,128)S(1)}, u32[]{:S(2)}, u32[]{:S(2)}) collective-permute-start(f32[2,10,32,1]{3,2,1,0:T(8,128)S(1)} %get-tuple-element.141), channel_id=1, source_target_pairs={{0,16},{16,32},{32,48},{48,64},{64,80},{80,96},{96,112},{112,128},... | collective-permute-start | bytes 7688 | tf_op jit(solution)/shard_map/ppermute | solution.py:17
  305.2 5.4 %collective-permute-done.42 = f32[2,10,32,1]{3,2,1,0:T(8,128)S(1)} collective-permute-done((f32[2,10,32,1]{3,2,1,0:T(8,128)S(1)}, f32[2,10,32,1]{3,2,1,0:T(8,128)S(1)}, u32[]{:S(2)}, u32[]{:S(2)}) %collective-permute-start.42) | collective-permute-done | bytes 2592 | tf_op jit(solution)/shard_map/ppermute | solution.py:17
  310.6 3.8 %collective-permute-done.43 = f32[2,10,32,1]{3,2,1,0:T(8,128)S(1)} collective-permute-done((f32[2,10,32,1]{3,2,1,0:T(8,128)S(1)}, f32[2,10,32,1]{3,2,1,0:T(8,128)S(1)}, u32[]{:S(2)}, u32[]{:S(2)}) %collective-permute-start.43) | collective-permute-done | bytes 2592 | tf_op jit(solution)/shard_map/ppermute | solution.py:20
  323.8 4.9 %collective-permute-start.47 = (f32[2,1,34,258]{3,2,1,0:T(8,128)S(1)}, f32[2,1,34,258]{3,2,1,0:T(8,128)S(1)}, u32[]{:S(2)}, u32[]{:S(2)}) collective-permute-start(f32[2,1,34,258]{3,2,1,0:T(8,128)S(1)} %get-tuple-element.118), channel_id=1, source_target_pairs={{1,0},{3,2},{5,4},{7,6},{9,8},{11,10},{13,12},{15,14},{17,16},{19,... | collective-permute-start | bytes 210536 | tf_op jit(solution)/shard_map/ppermute | solution.py:20
  (167 shorter events, 123.1 us)
Async XLA Ops:
  3.1 13.8 %collective-permute-start = (f32[3,10,32,1]{3,2,1,0:T(8,128)S(1)}, f32[3,10,32,1]{3,2,1,0:T(8,128)S(1)}, u32[]{:S(2)}, u32[]{:S(2)}) collective-permute-start(f32[3,10,32,1]{3,2,1,0:T(8,128)S(1)} %get-tuple-element.133), channel_id=1, source_target_pairs={{0,16},{16,32},{32,48},{48,64},{64,80},{80,96},{96,112},{112,128},... | collective-permute-start | bytes 11528 | tf_op jit(solution)/shard_map/ppermute | solution.py:17
  7.1 13.7 %collective-permute-start.1 = (f32[3,10,32,1]{3,2,1,0:T(8,128)S(1)}, f32[3,10,32,1]{3,2,1,0:T(8,128)S(1)}, u32[]{:S(2)}, u32[]{:S(2)}) collective-permute-start(f32[3,10,32,1]{3,2,1,0:T(8,128)S(1)} %get-tuple-element.134), channel_id=1, source_target_pairs={{16,0},{32,16},{48,32},{64,48},{80,64},{96,80},{112,96},{128,112},... | collective-permute-start | bytes 11528 | tf_op jit(solution)/shard_map/ppermute | solution.py:20
  29.8 6.3 %collective-permute-start.4 = (f32[3,1,34,258]{3,2,1,0:T(8,128)S(1)}, f32[3,1,34,258]{3,2,1,0:T(8,128)S(1)}, u32[]{:S(2)}, u32[]{:S(2)}) collective-permute-start(f32[3,1,34,258]{3,2,1,0:T(8,128)S(1)} %get-tuple-element.105), channel_id=1, source_target_pairs={{0,1},{2,3},{4,5},{6,7},{8,9},{10,11},{12,13},{14,15},{16,17},{18,... | collective-permute-start | bytes 315800 | tf_op jit(solution)/shard_map/ppermute | solution.py:17
  31.1 6.1 %collective-permute-start.5 = (f32[3,1,34,258]{3,2,1,0:T(8,128)S(1)}, f32[3,1,34,258]{3,2,1,0:T(8,128)S(1)}, u32[]{:S(2)}, u32[]{:S(2)}) collective-permute-start(f32[3,1,34,258]{3,2,1,0:T(8,128)S(1)} %get-tuple-element.106), channel_id=1, source_target_pairs={{1,0},{3,2},{5,4},{7,6},{9,8},{11,10},{13,12},{15,14},{17,16},{19,... | collective-permute-start | bytes 315800 | tf_op jit(solution)/shard_map/ppermute | solution.py:20
  40.5 6.3 %collective-permute-start.6 = (f32[10,32,1]{2,1,0:T(8,128)S(1)}, f32[10,32,1]{2,1,0:T(8,128)S(1)}, u32[]{:S(2)}, u32[]{:S(2)}) collective-permute-start(f32[10,32,1]{2,1,0:T(8,128)S(1)} %get-tuple-element.159), channel_id=1, source_target_pairs={{0,16},{16,32},{32,48},{48,64},{64,80},{80,96},{96,112},{112,128},... | collective-permute-start | bytes 3848 | tf_op jit(solution)/shard_map/ppermute | solution.py:17
  43.6 7.0 %collective-permute-start.7 = (f32[10,32,1]{2,1,0:T(8,128)S(1)}, f32[10,32,1]{2,1,0:T(8,128)S(1)}, u32[]{:S(2)}, u32[]{:S(2)}) collective-permute-start(f32[10,32,1]{2,1,0:T(8,128)S(1)} %get-tuple-element.160), channel_id=1, source_target_pairs={{16,0},{32,16},{48,32},{64,48},{80,64},{96,80},{112,96},{128,112},... | collective-permute-start | bytes 3848 | tf_op jit(solution)/shard_map/ppermute | solution.py:20
  54.3 5.8 %collective-permute-start.9 = (f32[10,1,258]{2,1,0:T(1,128)S(1)}, f32[10,1,258]{2,1,0:T(1,128)S(1)}, u32[]{:S(2)}, u32[]{:S(2)}) collective-permute-start(f32[10,1,258]{2,1,0:T(1,128)S(1)} %get-tuple-element.154), channel_id=1, source_target_pairs={{2,0},{4,2},{6,4},{8,6},{10,8},{12,10},{14,12},{3,1},{5,3},{7,5},{... | collective-permute-start | bytes 30968 | tf_op jit(solution)/shard_map/ppermute | solution.py:20
  60.2 5.9 %collective-permute-start.10 = (f32[1,34,258]{2,1,0:T(8,128)S(1)}, f32[1,34,258]{2,1,0:T(8,128)S(1)}, u32[]{:S(2)}, u32[]{:S(2)}) collective-permute-start(f32[1,34,258]{2,1,0:T(8,128)S(1)} %get-tuple-element.139), channel_id=1, source_target_pairs={{0,1},{2,3},{4,5},{6,7},{8,9},{10,11},{12,13},{14,15},{16,17},{18,... | collective-permute-start | bytes 105272 | tf_op jit(solution)/shard_map/ppermute | solution.py:17
  68.2 7.9 %collective-permute-start.12 = (f32[10,32,1]{2,1,0:T(8,128)S(1)}, f32[10,32,1]{2,1,0:T(8,128)S(1)}, u32[]{:S(2)}, u32[]{:S(2)}) collective-permute-start(f32[10,32,1]{2,1,0:T(8,128)S(1)} %get-tuple-element.157), channel_id=1, source_target_pairs={{0,16},{16,32},{32,48},{48,64},{64,80},{80,96},{96,112},{112,128},... | collective-permute-start | bytes 3848 | tf_op jit(solution)/shard_map/ppermute | solution.py:17
  72.9 7.0 %collective-permute-start.13 = (f32[10,32,1]{2,1,0:T(8,128)S(1)}, f32[10,32,1]{2,1,0:T(8,128)S(1)}, u32[]{:S(2)}, u32[]{:S(2)}) collective-permute-start(f32[10,32,1]{2,1,0:T(8,128)S(1)} %get-tuple-element.158), channel_id=1, source_target_pairs={{16,0},{32,16},{48,32},{64,48},{80,64},{96,80},{112,96},{128,112},... | collective-permute-start | bytes 3848 | tf_op jit(solution)/shard_map/ppermute | solution.py:20
  80.0 6.2 %collective-permute-start.14 = (f32[10,1,258]{2,1,0:T(1,128)S(1)}, f32[10,1,258]{2,1,0:T(1,128)S(1)}, u32[]{:S(2)}, u32[]{:S(2)}) collective-permute-start(f32[10,1,258]{2,1,0:T(1,128)S(1)} %get-tuple-element.151), channel_id=1, source_target_pairs={{0,2},{2,4},{4,6},{6,8},{8,10},{10,12},{12,14},{1,3},{3,5},{5,7},{... | collective-permute-start | bytes 30968 | tf_op jit(solution)/shard_map/ppermute | solution.py:17
  89.8 5.9 %collective-permute-start.16 = (f32[1,34,258]{2,1,0:T(8,128)S(1)}, f32[1,34,258]{2,1,0:T(8,128)S(1)}, u32[]{:S(2)}, u32[]{:S(2)}) collective-permute-start(f32[1,34,258]{2,1,0:T(8,128)S(1)} %get-tuple-element.137), channel_id=1, source_target_pairs={{0,1},{2,3},{4,5},{6,7},{8,9},{10,11},{12,13},{14,15},{16,17},{18,... | collective-permute-start | bytes 105272 | tf_op jit(solution)/shard_map/ppermute | solution.py:17
  99.1 7.6 %collective-permute-start.18 = (f32[10,32,1]{2,1,0:T(8,128)}, f32[10,32,1]{2,1,0:T(8,128)}, u32[]{:S(2)}, u32[]{:S(2)}) collective-permute-start(f32[10,32,1]{2,1,0:T(8,128)} %get-tuple-element.155), channel_id=1, source_target_pairs={{0,16},{16,32},{32,48},{48,64},{64,80},{80,96},{96,112},{112,128},... | collective-permute-start | bytes 3848 | tf_op jit(solution)/shard_map/ppermute | solution.py:17
  103.8 7.3 %collective-permute-start.19 = (f32[10,32,1]{2,1,0:T(8,128)}, f32[10,32,1]{2,1,0:T(8,128)}, u32[]{:S(2)}, u32[]{:S(2)}) collective-permute-start(f32[10,32,1]{2,1,0:T(8,128)} %get-tuple-element.156), channel_id=1, source_target_pairs={{16,0},{32,16},{48,32},{64,48},{80,64},{96,80},{112,96},{128,112},... | collective-permute-start | bytes 3848 | tf_op jit(solution)/shard_map/ppermute | solution.py:20
  112.8 6.9 %collective-permute-start.20 = (f32[10,1,258]{2,1,0:T(1,128)}, f32[10,1,258]{2,1,0:T(1,128)}, u32[]{:S(2)}, u32[]{:S(2)}) collective-permute-start(f32[10,1,258]{2,1,0:T(1,128)} %get-tuple-element.149), channel_id=1, source_target_pairs={{0,2},{2,4},{4,6},{6,8},{8,10},{10,12},{12,14},{1,3},{3,5},{5,7},{... | collective-permute-start | bytes 30968 | tf_op jit(solution)/shard_map/ppermute | solution.py:17
  122.8 8.2 %collective-permute-start.22 = (f32[1,34,258]{2,1,0:T(8,128)S(1)}, f32[1,34,258]{2,1,0:T(8,128)S(1)}, u32[]{:S(2)}, u32[]{:S(2)}) collective-permute-start(f32[1,34,258]{2,1,0:T(8,128)S(1)} %get-tuple-element.135), channel_id=1, source_target_pairs={{0,1},{2,3},{4,5},{6,7},{8,9},{10,11},{12,13},{14,15},{16,17},{18,... | collective-permute-start | bytes 105272 | tf_op jit(solution)/shard_map/ppermute | solution.py:17
  124.1 6.9 %collective-permute-start.23 = (f32[1,34,258]{2,1,0:T(8,128)S(1)}, f32[1,34,258]{2,1,0:T(8,128)S(1)}, u32[]{:S(2)}, u32[]{:S(2)}) collective-permute-start(f32[1,34,258]{2,1,0:T(8,128)S(1)} %get-tuple-element.136), channel_id=1, source_target_pairs={{1,0},{3,2},{5,4},{7,6},{9,8},{11,10},{13,12},{15,14},{17,16},{19,... | collective-permute-start | bytes 105272 | tf_op jit(solution)/shard_map/ppermute | solution.py:20
  208.0 8.4 %collective-permute-start.24 = (f32[2,10,32,1]{3,2,1,0:T(8,128)S(1)}, f32[2,10,32,1]{3,2,1,0:T(8,128)S(1)}, u32[]{:S(2)}, u32[]{:S(2)}) collective-permute-start(f32[2,10,32,1]{3,2,1,0:T(8,128)S(1)} %get-tuple-element.147), channel_id=1, source_target_pairs={{0,16},{16,32},{32,48},{48,64},{64,80},{80,96},{96,112},{112,128},... | collective-permute-start | bytes 7688 | tf_op jit(solution)/shard_map/ppermute | solution.py:17
  209.3 10.9 %collective-permute-start.25 = (f32[2,10,32,1]{3,2,1,0:T(8,128)S(1)}, f32[2,10,32,1]{3,2,1,0:T(8,128)S(1)}, u32[]{:S(2)}, u32[]{:S(2)}) collective-permute-start(f32[2,10,32,1]{3,2,1,0:T(8,128)S(1)} %get-tuple-element.148), channel_id=1, source_target_pairs={{16,0},{32,16},{48,32},{64,48},{80,64},{96,80},{112,96},{128,112},... | collective-permute-start | bytes 7688 | tf_op jit(solution)/shard_map/ppermute | solution.py:20
  227.5 5.8 %collective-permute-start.28 = (f32[2,1,34,258]{3,2,1,0:T(8,128)S(1)}, f32[2,1,34,258]{3,2,1,0:T(8,128)S(1)}, u32[]{:S(2)}, u32[]{:S(2)}) collective-permute-start(f32[2,1,34,258]{3,2,1,0:T(8,128)S(1)} %get-tuple-element.123), channel_id=1, source_target_pairs={{0,1},{2,3},{4,5},{6,7},{8,9},{10,11},{12,13},{14,15},{16,17},{18,... | collective-permute-start | bytes 210536 | tf_op jit(solution)/shard_map/ppermute | solution.py:17
  238.3 8.2 %collective-permute-start.30 = (f32[2,10,32,1]{3,2,1,0:T(8,128)S(1)}, f32[2,10,32,1]{3,2,1,0:T(8,128)S(1)}, u32[]{:S(2)}, u32[]{:S(2)}) collective-permute-start(f32[2,10,32,1]{3,2,1,0:T(8,128)S(1)} %get-tuple-element.145), channel_id=1, source_target_pairs={{0,16},{16,32},{32,48},{48,64},{64,80},{80,96},{96,112},{112,128},... | collective-permute-start | bytes 7688 | tf_op jit(solution)/shard_map/ppermute | solution.py:17
  239.6 10.6 %collective-permute-start.31 = (f32[2,10,32,1]{3,2,1,0:T(8,128)S(1)}, f32[2,10,32,1]{3,2,1,0:T(8,128)S(1)}, u32[]{:S(2)}, u32[]{:S(2)}) collective-permute-start(f32[2,10,32,1]{3,2,1,0:T(8,128)S(1)} %get-tuple-element.146), channel_id=1, source_target_pairs={{16,0},{32,16},{48,32},{64,48},{80,64},{96,80},{112,96},{128,112},... | collective-permute-start | bytes 7688 | tf_op jit(solution)/shard_map/ppermute | solution.py:20
  258.2 6.0 %collective-permute-start.34 = (f32[2,1,34,258]{3,2,1,0:T(8,128)S(1)}, f32[2,1,34,258]{3,2,1,0:T(8,128)S(1)}, u32[]{:S(2)}, u32[]{:S(2)}) collective-permute-start(f32[2,1,34,258]{3,2,1,0:T(8,128)S(1)} %get-tuple-element.121), channel_id=1, source_target_pairs={{0,1},{2,3},{4,5},{6,7},{8,9},{10,11},{12,13},{14,15},{16,17},{18,... | collective-permute-start | bytes 210536 | tf_op jit(solution)/shard_map/ppermute | solution.py:17
  259.5 5.7 %collective-permute-start.35 = (f32[2,1,34,258]{3,2,1,0:T(8,128)S(1)}, f32[2,1,34,258]{3,2,1,0:T(8,128)S(1)}, u32[]{:S(2)}, u32[]{:S(2)}) collective-permute-start(f32[2,1,34,258]{3,2,1,0:T(8,128)S(1)} %get-tuple-element.122), channel_id=1, source_target_pairs={{1,0},{3,2},{5,4},{7,6},{9,8},{11,10},{13,12},{15,14},{17,16},{19,... | collective-permute-start | bytes 210536 | tf_op jit(solution)/shard_map/ppermute | solution.py:20
  269.1 8.9 %collective-permute-start.36 = (f32[2,10,32,1]{3,2,1,0:T(8,128)S(1)}, f32[2,10,32,1]{3,2,1,0:T(8,128)S(1)}, u32[]{:S(2)}, u32[]{:S(2)}) collective-permute-start(f32[2,10,32,1]{3,2,1,0:T(8,128)S(1)} %get-tuple-element.143), channel_id=1, source_target_pairs={{0,16},{16,32},{32,48},{48,64},{64,80},{80,96},{96,112},{112,128},... | collective-permute-start | bytes 7688 | tf_op jit(solution)/shard_map/ppermute | solution.py:17
  271.3 10.5 %collective-permute-start.37 = (f32[2,10,32,1]{3,2,1,0:T(8,128)S(1)}, f32[2,10,32,1]{3,2,1,0:T(8,128)S(1)}, u32[]{:S(2)}, u32[]{:S(2)}) collective-permute-start(f32[2,10,32,1]{3,2,1,0:T(8,128)S(1)} %get-tuple-element.144), channel_id=1, source_target_pairs={{16,0},{32,16},{48,32},{64,48},{80,64},{96,80},{112,96},{128,112},... | collective-permute-start | bytes 7688 | tf_op jit(solution)/shard_map/ppermute | solution.py:20
  289.7 6.2 %collective-permute-start.40 = (f32[2,1,34,258]{3,2,1,0:T(8,128)S(1)}, f32[2,1,34,258]{3,2,1,0:T(8,128)S(1)}, u32[]{:S(2)}, u32[]{:S(2)}) collective-permute-start(f32[2,1,34,258]{3,2,1,0:T(8,128)S(1)} %get-tuple-element.119), channel_id=1, source_target_pairs={{0,1},{2,3},{4,5},{6,7},{8,9},{10,11},{12,13},{14,15},{16,17},{18,... | collective-permute-start | bytes 210536 | tf_op jit(solution)/shard_map/ppermute | solution.py:17
  291.0 5.8 %collective-permute-start.41 = (f32[2,1,34,258]{3,2,1,0:T(8,128)S(1)}, f32[2,1,34,258]{3,2,1,0:T(8,128)S(1)}, u32[]{:S(2)}, u32[]{:S(2)}) collective-permute-start(f32[2,1,34,258]{3,2,1,0:T(8,128)S(1)} %get-tuple-element.120), channel_id=1, source_target_pairs={{1,0},{3,2},{5,4},{7,6},{9,8},{11,10},{13,12},{15,14},{17,16},{19,... | collective-permute-start | bytes 210536 | tf_op jit(solution)/shard_map/ppermute | solution.py:20
  299.9 10.7 %collective-permute-start.42 = (f32[2,10,32,1]{3,2,1,0:T(8,128)S(1)}, f32[2,10,32,1]{3,2,1,0:T(8,128)S(1)}, u32[]{:S(2)}, u32[]{:S(2)}) collective-permute-start(f32[2,10,32,1]{3,2,1,0:T(8,128)S(1)} %get-tuple-element.141), channel_id=1, source_target_pairs={{0,16},{16,32},{32,48},{48,64},{64,80},{80,96},{96,112},{112,128},... | collective-permute-start | bytes 7688 | tf_op jit(solution)/shard_map/ppermute | solution.py:17
  303.9 10.5 %collective-permute-start.43 = (f32[2,10,32,1]{3,2,1,0:T(8,128)S(1)}, f32[2,10,32,1]{3,2,1,0:T(8,128)S(1)}, u32[]{:S(2)}, u32[]{:S(2)}) collective-permute-start(f32[2,10,32,1]{3,2,1,0:T(8,128)S(1)} %get-tuple-element.142), channel_id=1, source_target_pairs={{16,0},{32,16},{48,32},{64,48},{80,64},{96,80},{112,96},{128,112},... | collective-permute-start | bytes 7688 | tf_op jit(solution)/shard_map/ppermute | solution.py:20
  322.3 7.0 %collective-permute-start.46 = (f32[2,1,34,258]{3,2,1,0:T(8,128)S(1)}, f32[2,1,34,258]{3,2,1,0:T(8,128)S(1)}, u32[]{:S(2)}, u32[]{:S(2)}) collective-permute-start(f32[2,1,34,258]{3,2,1,0:T(8,128)S(1)} %get-tuple-element.117), channel_id=1, source_target_pairs={{0,1},{2,3},{4,5},{6,7},{8,9},{10,11},{12,13},{14,15},{16,17},{18,... | collective-permute-start | bytes 210536 | tf_op jit(solution)/shard_map/ppermute | solution.py:17
  323.8 5.8 %collective-permute-start.47 = (f32[2,1,34,258]{3,2,1,0:T(8,128)S(1)}, f32[2,1,34,258]{3,2,1,0:T(8,128)S(1)}, u32[]{:S(2)}, u32[]{:S(2)}) collective-permute-start(f32[2,1,34,258]{3,2,1,0:T(8,128)S(1)} %get-tuple-element.118), channel_id=1, source_target_pairs={{1,0},{3,2},{5,4},{7,6},{9,8},{11,10},{13,12},{15,14},{17,16},{19,... | collective-permute-start | bytes 210536 | tf_op jit(solution)/shard_map/ppermute | solution.py:20
  (31 other events, 465.8 us)
where the time goes:
time: 338 us; the launch traced here: 335 us
  starting transfers between devices  122 us (36%)
  waiting for transfers between devices  99.9 us (30%)
  blocking collectives  73.8 us (22%)
  other arithmetic  29.9 us (9%)
  local copies, waits for them, and re-layouts  7.67 us (2%)
    ppermute x24, waiting for transfers between devices, extended(): lax.ppermute(lax.slice_in_dim(block, 0, width, axis=dim), axis, backward)  63.9 us
    ppermute x24, starting transfers between devices, extended(): lax.ppermute(lax.slice_in_dim(block, block.shape[dim] - width, None, axis...  62.8 us
    ppermute x24, starting transfers between devices, extended(): lax.ppermute(lax.slice_in_dim(block, 0, width, axis=dim), axis, backward)  58.7 us
    psum x1, blocking collectives, shards(): zonal_all = lax.psum(zonal, 'lon')  57.3 us
    ppermute x24, waiting for transfers between devices, extended(): lax.ppermute(lax.slice_in_dim(block, block.shape[dim] - width, None, axis...  36.1 us
    all_gather x2, blocking collectives, carried_in(): gathered = lax.all_gather(part, axis)  16.5 us
  transfers between devices with their start and end apart: 48, of which 31 were waited for; matrix products, arithmetic and copies ran while one was open for 1% of the time, Pallas kernels for 0%

commit v1 on v0

v1 whole, which is shorter than its diff:
```python
import functools
import math

import jax
import jax.numpy as jnp
from jax import lax
from jax.experimental import pallas as pl
from jax.experimental.pallas import tpu as pltpu
from jax.sharding import PartitionSpec as P

MESH = pl.DeviceIdType.MESH
diffusion_step = 0.08
cubic_drag = 0.15

HALO = 4


def stencil(couple, value, level, levels):
    here = couple[level] * value[level]
    return around(here, couple[level - 1] * value[level - 1] if level else None, couple[level + 1] * value[level + 1])


def around(here, before, after):
    rows, columns = here.shape
    total = pltpu.roll(here, 1, 1) + pltpu.roll(here, columns - 1, 1)
    total = total + (pltpu.roll(here, 1, 0) + pltpu.roll(here, rows - 1, 0))
    total = total + (after if before is None else before + after)
    return total


def kernel(
    n_lon, n_lat, n_depth, scale, grid_scale,
    states, direction, mixing, level_dz, lat_width, cost_weight, ocean, atlantic, levels_in,
    hess, grad, overturning,
    st_states, st_dir, st_mix, st_ocean, st_atl, st_lev,
    fields, capacity, tan1, tan2, tan3, tan4, tan3_wide, lam, mu,
    flat, strips_out, strips_in, strip3_out, strip3_in, dz_out, dz_in, zone, zones, totals, prefixes, weights,
    in_sem, lat_send, lat_recv, lon_send, lon_recv, diag_send, diag_recv, dep_send, dep_recv,
    zone_send, zone_recv, tot_send, tot_recv, t3_send, t3_recv,
):
    layers, rows, columns = direction.shape
    all_layers = 2 * layers
    ext_rows, ext_columns = fields.shape[-2:]
    lon, lat, dep = lax.axis_index("lon"), lax.axis_index("lat"), lax.axis_index("depth")
    wrap = lambda value, size: lax.rem(value + size, size)

    def at(dl=0, dz=0, dd=0):
        return (wrap(lon + dl, n_lon), wrap(lat + dz, n_lat), wrap(dep + dd, n_depth))

    plane = [(i, d) for d in range(n_depth) for i in range(n_lon) if i or d]
    peers = [at(dl=i, dd=d) for i, d in plane] + [at(dz=z) for z in (1, -1)]
    peers += [at(dl=x, dz=z) for x in (1, -1) for z in (1, -1)]
    barrier = pltpu.get_barrier_semaphore()
    for peer in peers:
        pl.semaphore_signal(barrier, inc=1, device_id=peer, device_id_type=MESH)

    loads = [
        pltpu.make_async_copy(src, dst, in_sem.at[i])
        for i, (src, dst) in enumerate((
            (levels_in, st_lev), (ocean, st_ocean), (atlantic, st_atl), (mixing, st_mix),
            (direction, st_dir), (states, st_states),
        ))
    ]
    for load in loads:
        load.start()

    sends = []

    def send(src, dst, send_sem, recv_sem, device):
        copy = pltpu.make_async_remote_copy(
            src_ref=src, dst_ref=dst, send_sem=send_sem, recv_sem=recv_sem, device_id=device, device_id_type=MESH
        )
        copy.start()
        sends.append(copy)
        return copy

    upright = dep == 0
    own = lambda j: jnp.where(upright, j, layers - 1 - j)
    lane = lax.broadcasted_iota(jnp.int32, (rows, 128), 1)
    group = lane // HALO
    row = lax.broadcasted_iota(jnp.int32, (rows, 128), 0)

    width = jnp.zeros((rows, 128), jnp.float32)
    for r in range(rows):
        width = jnp.where(row == r, lat_width[r], width)
    square_row = lax.broadcasted_iota(jnp.int32, (rows, rows), 0)
    square_lane = lax.broadcasted_iota(jnp.int32, (rows, rows), 1)
    by_level = jnp.zeros((rows, 128), jnp.float32)
    for k in range(all_layers):
        line = cost_weight[pl.ds(jnp.where(upright, k, all_layers - 1 - k), 1), :]
        column = jnp.sum(jnp.where(square_row == square_lane, line, 0.0), axis=1, keepdims=True)
        by_level = jnp.where(lane == k, column * grid_scale, by_level)
    flat[0:rows, 0:128] = by_level
    dz_out[...] = jnp.zeros(dz_out.shape, jnp.float32) + level_dz[own(layers - 1)] * scale

    for load in loads:
        load.wait()
    basin = st_atl[...].astype(jnp.float32) * jnp.concatenate([width] * (columns // 128), axis=1)
    flat[0:rows, 128 : 128 + columns] = basin
    reach = st_lev[...] * st_ocean[...]

    edge = columns - 128
    packed = [[jnp.zeros((rows, 128), jnp.float32)] * 2 for _ in range(2)]

    def pack(pair, block, slot):
        right = pltpu.roll(block[:, edge:], (HALO * slot) % 128, 1)
        left = pltpu.roll(block[:, :128], (HALO * slot) % 128, 1)
        pair[0] = jnp.where(group == (slot - 1) % 32, right, pair[0])
        pair[1] = jnp.where(group == slot, left, pair[1])

    pack(packed[0], basin, 3 * layers)
    for j in range(layers):
        k = own(j)
        wet = dep * layers + k < reach
        couple = jnp.where(wet, math.sqrt(diffusion_step) * st_mix[k], 0.0)
        parts = [couple, st_dir[k]]
        parts += [jnp.where(wet, math.sqrt(3.0 * cubic_drag) * st_states[s, k], 0.0) for s in range(4)]
        for f, part in enumerate(parts):
            fields[f, j, 0:rows, 0:columns] = part
            pack(packed[f // 3], part, (f % 3) * layers + j)
    for m in range(2):
        for way in range(2):
            strips_out[m, way] = packed[m][way]

    pl.semaphore_wait(barrier, len(peers))

    arrivals = []
    near, far = slice(0, HALO), slice(rows - HALO, rows)
    below, above = slice(rows, rows + HALO), slice(rows + HALO, rows + 2 * HALO)

    def send_rows(ref, lead, lanes, first):
        a = send(ref.at[lead + (near, lanes)], ref.at[lead + (below, lanes)], lat_send.at[first], lat_recv.at[first], at(dz=-1))
        b = send(ref.at[lead + (far, lanes)], ref.at[lead + (above, lanes)], lat_send.at[first + 1], lat_recv.at[first + 1], at(dz=1))
        arrivals.extend((a, b))

    def send_strips(m):
        for way, dl in ((0, 1), (1, -1)):
            i = 2 * m + way
            arrivals.append(send(strips_out.at[m, way], strips_in.at[m, way, 0:rows], lon_send.at[i], lon_recv.at[i], at(dl=dl)))
            for up, (src, dst, dz) in enumerate(((near, below, -1), (far, above, 1))):
                i2 = 2 * i + up
                arrivals.append(send(strips_out.at[m, way, src], strips_in.at[m, way, dst], diag_send.at[i2], diag_recv.at[i2], at(dl=dl, dz=dz)))

    send_strips(0)
    send_rows(fields, (slice(0, 3), slice(0, layers)), slice(0, columns), 0)
    send_rows(flat, (), slice(0, 128 + columns), 2)
    send_strips(1)
    send_rows(fields, (slice(3, 6), slice(0, layers)), slice(0, columns), 4)
    dz_copy = send(dz_out, dz_in, dep_send.at[0], dep_recv.at[0], at(dd=1))
    for copy in arrivals:
        copy.wait_recv()

    lane_x = lax.broadcasted_iota(jnp.int32, (ext_rows, 128), 1)
    even = (lane_x // HALO) % 2 == 0

    def combine(pair):
        from_left, from_right = pair[0], pair[1]
        return [jnp.where(even, from_right, from_left), jnp.where(even, from_left, from_right)]

    def unpack(both, slot):
        return pltpu.roll(both[slot % 2], (128 - HALO * slot) % 128, 1)

    one = lambda flag: jnp.where(flag, 1.0, 0.0).astype(jnp.float32)
    lane_mask = jnp.where(lane_x < HALO, one(lon < n_lon - 1), jnp.where(lane_x >= 128 - HALO, one(lon > 0), 0.0))
    row_8 = lax.broadcasted_iota(jnp.int32, (2 * HALO, ext_columns), 0)
    row_mask = jnp.where(row_8 < HALO, one(lat < n_lat - 1), one(lat > 0))
    for m in range(2):
        both = combine(strips_in[m])
        for f in range(3):
            for j in range(layers):
                halo = unpack(both, f * layers + j)
                if m == 0 and f == 0:
                    halo = halo * lane_mask
                fields[3 * m + f, j, :, columns:] = halo
        if m == 0:
            flat[:, 128 + columns :] = unpack(both, 3 * layers)
    couple = fields.at[0]
    for j in range(layers):
        couple[j, rows:, :] = couple[j, rows:, :] * row_mask

    def send_level(ref, i):
        return send(ref.at[layers - 1], ref.at[layers], dep_send.at[i], dep_recv.at[i], at(dd=1))

    border = [send_level(fields.at[f], i) for f, i in ((0, 1), (1, 2), (5, 3))]

    tangents = [fields.at[1], tan1, tan2, tan3]
    drag = [fields.at[2 + s] for s in range(4)]

    def capacity_at(j):
        here = couple[j]
        total = around(here, couple[j - 1] if j else None, couple[j + 1])
        capacity[j] = jnp.where(here > 0.0, 1.0, 0.0) - here * total

    def tangent_at(s, j, out):
        value = tangents[s]
        damp = drag[s][j]
        return couple[j] * stencil(couple, value, j, layers) + (capacity[j] - damp * damp) * value[j]

    for j in range(layers - 1):
        capacity_at(j)
    for j in range(layers - 1):
        tan1[j] = tangent_at(0, j, None)
    for copy in border:
        copy.wait_recv()
    capacity_at(layers - 1)
    tan1[layers - 1] = tangent_at(0, layers - 1, None)
    pending = send_level(tan1, 4)

    def zonal(block, j):
        weighted = block[0:rows, 0:columns] * flat[0:rows, 128 : 128 + columns]
        folded = weighted[:, 0:128]
        for part in range(1, columns // 128):
            folded = folded + weighted[:, 128 * part : 128 * part + 128]
        return jnp.sum(folded, axis=1, keepdims=True) * (level_dz[own(j)] * scale)

    tiles = rows // 8
    lane_8 = lax.broadcasted_iota(jnp.int32, (8, 128), 1)
    sums = jnp.zeros((8, 128), jnp.float32)

    def put(sums, column, f, j):
        for t in range(tiles):
            slot = t * 2 * layers + f * layers + j
            sums = jnp.where(lane_8 == slot, column[8 * t : 8 * t + 8], sums)
        return sums

    last = drag[3]
    for j in range(layers):
        here = last[j]
        final = couple[j] * stencil(couple, last, j, layers) + (capacity[j] - here * here * (1.0 / 3.0)) * here
        sums = put(sums, zonal(final, j) * (1.0 / math.sqrt(3.0 * cubic_drag)), 0, j)

    for s in (1, 2):
        nxt = tangents[s + 1]
        for j in range(layers):
            if j == layers - 1:
                pending.wait_recv()
            nxt[j] = tangent_at(s, j, None)
        pending = send_level(nxt, 4 + s)

    pair = [jnp.zeros((rows, 128), jnp.float32)] * 2
    for j in range(layers):
        tan3_wide[j, 0:rows, 0:columns] = tan3[j, 0:rows, 0:columns]
        pack(pair, tan3[j, 0:rows, 0:columns], j)
    strip3_out[0] = pair[0]
    strip3_out[1] = pair[1]
    third = []
    for way, dl in ((0, 1), (1, -1)):
        third.append(send(strip3_out.at[way], strip3_in.at[way, 0:rows], t3_send.at[way], t3_recv.at[way], at(dl=dl)))
        for up, (src, dst, dz) in enumerate(((near, below, -1), (far, above, 1))):
            i = 2 + 2 * way + up
            third.append(send(strip3_out.at[way, src], strip3_in.at[way, dst], t3_send.at[i], t3_recv.at[i], at(dl=dl, dz=dz)))
    every = slice(0, layers)
    own_lanes = slice(0, columns)
    for i, (src, dst, dz) in enumerate(((near, below, -1), (far, above, 1))):
        third.append(send(tan3_wide.at[every, src, own_lanes], tan3_wide.at[every, dst, own_lanes], t3_send.at[6 + i], t3_recv.at[6 + i], at(dz=dz)))

    for j in range(layers):
        if j == layers - 1:
            pending.wait_recv()
        sums = put(sums, zonal(tangent_at(3, j, None), j), 1, j)

    zone[...] = sums
    zones[lon] = sums
    gathered = []
    for i, (dl, dd) in enumerate(plane):
        slot = lon + (n_lon if dd else 0)
        gathered.append(send(zone, zones.at[slot], zone_send.at[i], zone_recv.at[i], at(dl=dl, dd=dd)))

    for copy in third:
        copy.wait_recv()
    both = combine(strip3_in)
    for j in range(layers):
        tan3_wide[j, :, columns:] = unpack(both, j)
    for k in range(all_layers):
        weights[k] = jnp.broadcast_to(flat[:, k : k + 1], (ext_rows, 128))
    dz_copy.wait_recv()

    for copy in gathered:
        copy.wait_recv()
    mine = zones[0]
    other = zones[n_lon]
    for i in range(1, n_lon):
        mine = mine + zones[i]
        other = other + zones[n_lon + i]
    for t in range(tiles):
        shift = (128 - 2 * layers * t) % 128
        a = pltpu.roll(mine, shift, 1) if shift else mine
        b = pltpu.roll(other, (shift + 2 * layers) % 128, 1)
        totals[8 * t : 8 * t + 8] = jnp.where(lane_8 < 2 * layers, a, b)
    border = [
        send(totals.at[src], totals.at[dst], tot_send.at[i], tot_recv.at[i], at(dz=dz))
        for i, (src, dst, dz) in enumerate(((near, below, -1), (far, above, 1)))
    ]

    def place(f, k):
        if k < layers:
            return f * layers + k
        return 2 * layers + f * layers + (all_layers - 1 - k)

    def prefix_rows(part):
        count = part.stop - part.start
        streams = []
        for f in range(2):
            terms = [jnp.broadcast_to(totals[part, place(f, k) : place(f, k) + 1], (count, 128)) for k in range(all_layers)]
            stream = both_ways(terms, upright, False)
            if f == 0:
                streams = stream
            forced = [weights[k, part] * stream[k] for k in range(all_layers)]
            prefix = both_ways(forced, upright, True)
            for k in range(layers + 1):
                prefixes[f, k, part] = prefix[k]
        return streams

    streams = prefix_rows(slice(0, rows))
    spots = lax.broadcasted_iota(jnp.int32, (rows, rows), 0) == lax.broadcasted_iota(jnp.int32, (rows, rows), 1)
    for j in range(layers):
        line = jnp.sum(jnp.where(spots, streams[j][:, 0:rows], 0.0), axis=0, keepdims=True)
        overturning[pl.ds(own(j), 1), :] = line
    for copy in border:
        copy.wait_recv()
    prefix_rows(slice(rows, ext_rows))

    basin = flat[:, 128:]
    for j in range(layers + 1):
        if j < layers:
            area = basin * (level_dz[own(j)] * scale)
        else:
            area = basin * dz_in[0:1, 0:1]
        for f, ref in ((0, lam), (1, mu)):
            ref[0, j] = area * jnp.concatenate([prefixes[f, j]] * (ext_columns // 128), axis=1)

    ratio = 6.0 * cubic_drag / math.sqrt(3.0 * cubic_drag)
    pending = None
    for n, s in enumerate(reversed(range(4))):
        tangent = tan3_wide if s == 3 else tangents[s]
        for j in range(layers):
            if j == layers - 1 and pending is not None:
                for copy in pending:
                    copy.wait_recv()
            damp = drag[s][j]
            keep = capacity[j] - damp * damp
            here = lam[n, j]
            new_lam = couple[j] * stencil(couple, lam.at[n], j, layers) + keep * here
            new_mu = couple[j] * stencil(couple, mu.at[n], j, layers) + keep * mu[n, j]
            new_mu = new_mu - (ratio * damp) * (tangent[j] * here)
            if s:
                lam[n + 1, j] = new_lam
                mu[n + 1, j] = new_mu
            else:
                grad[own(j)] = new_lam[0:rows, 0:columns]
                hess[own(j)] = new_mu[0:rows, 0:columns]
        if s:
            pending = [send_level(lam.at[n + 1], 7 + 2 * n), send_level(mu.at[n + 1], 8 + 2 * n)]
    for copy in sends:
        copy.wait_send()


def both_ways(terms, upright, forward):
    count = len(terms)
    up = [terms[0]]
    for k in range(1, count):
        up.append(up[-1] + terms[k])
    down = [terms[-1]]
    for k in range(count - 2, -1, -1):
        down.append(down[-1] + terms[k])
    down = down[::-1]
    choose_up = upright if forward else jnp.logical_not(upright)
    return [jnp.where(choose_up, a, b) for a, b in zip(up, down)]


def solution(mesh):
    n_lon, n_lat, n_depth = (mesh.shape[name] for name in ("lon", "lat", "depth"))

    def shards(states, direction, mixing, level_dz, lat_width, cost_weight, ocean_columns, atlantic, levels):
        layers, rows, columns = direction.shape
        ext = (rows + 2 * HALO, columns + 128)
        tall = (layers + 1,) + ext
        f32, i32 = jnp.float32, jnp.int32
        vmem = lambda *shape: pltpu.VMEM(shape, f32)
        dma = lambda count: pltpu.SemaphoreType.DMA((count,))
        in_vmem, in_smem, anywhere = (pl.BlockSpec(memory_space=m) for m in (pltpu.VMEM, pltpu.SMEM, pl.ANY))
        scale = 1.0 / math.sqrt(columns * n_lon * layers * n_depth)
        body = functools.partial(kernel, n_lon, n_lat, n_depth, scale, math.sqrt(columns * n_lon))
        return pl.pallas_call(
            body,
            out_shape=(
                jax.ShapeDtypeStruct(direction.shape, f32),
                jax.ShapeDtypeStruct(direction.shape, f32),
                jax.ShapeDtypeStruct((layers, rows), f32),
            ),
            in_specs=[anywhere] * 3 + [in_smem] * 2 + [in_vmem] + [anywhere] * 3,
            out_specs=(in_vmem,) * 3,
            scratch_shapes=[
                vmem(*states.shape), vmem(*direction.shape), vmem(*direction.shape),
                pltpu.VMEM((rows, columns), i32), pltpu.VMEM((rows, columns), i32), pltpu.VMEM((rows, columns), i32),
                vmem(6, *tall), vmem(layers, *ext), vmem(*tall), vmem(*tall), vmem(*tall), vmem(8, 128),
                vmem(layers, *ext), vmem(4, *tall), vmem(4, *tall),
                vmem(ext[0], 128 + ext[1]), vmem(2, 2, rows, 128), vmem(2, 2, ext[0], 128),
                vmem(2, rows, 128), vmem(2, ext[0], 128), vmem(8, 128), vmem(8, 128),
                vmem(8, 128), vmem(2 * n_lon, 8, 128), vmem(ext[0], 128),
                vmem(2, layers + 1, ext[0], 128), vmem(n_depth * layers, ext[0], 128),
                dma(6), dma(6), dma(6), dma(4), dma(4), dma(8), dma(8), dma(16), dma(16),
                dma(2 * n_lon - 1), dma(2 * n_lon - 1), dma(2), dma(2), dma(8), dma(8),
            ],
            compiler_params=pltpu.CompilerParams(
                collective_id=0, has_side_effects=True, vmem_limit_bytes=48 * 2**20
            ),
            cost_estimate=pl.CostEstimate(flops=3 * 10**7, bytes_accessed=3 * 10**6, transcendentals=0),
        )(states, direction, mixing, level_dz, lat_width, cost_weight, ocean_columns, atlantic, levels)

    placed = (
        P(None, "depth", "lat", "lon"),
        P("depth", "lat", "lon"),
        P("depth", "lat", "lon"),
        P("depth"),
        P("lat"),
        P(None, "lat"),
        P("lat", "lon"),
        P("lat", "lon"),
        P("lat", "lon"),
    )
    return jax.shard_map(
        shards,
        mesh=mesh,
        in_specs=placed,
        out_specs=(P("depth", "lat", "lon"), P("depth", "lat", "lon"), P("depth", "lat")),
        check_vma=False,
    )
```

time: 338 us -> 50.9 us (0.15)
  starting transfers between devices: 122 us -> 0 us
  waiting for transfers between devices: 99.9 us -> 0 us
  blocking collectives: 73.8 us -> 0 us
  Pallas kernels: 0 us -> 40.2 us
  other arithmetic: 29.9 us -> 0 us
    ppermute x48 -> x0, starting transfers between devices: 122 us -> none  [the longest x24 62.8 us: extended(): lax.ppermute(lax.slice_in_dim(block, block.shape[dim] - width, None, axis...]
    ppermute x48 -> x0, waiting for transfers between devices: 99.9 us -> none  [the longest x24 63.9 us: extended(): lax.ppermute(lax.slice_in_dim(block, 0, width, axis=dim), axis, backward)]
    psum x1 -> x0, blocking collectives: 57.3 us -> none  [shards(): zonal_all = lax.psum(zonal, 'lon')]
    pallas_call x0 -> x1, Pallas kernels: none -> 40.2 us  [shards(): pl.pallas_call(body, out_shape=(jax.ShapeDtypeStruct(direction.shape, f32...]
    all_gather x2 -> x0, blocking collectives: 16.5 us -> none  [carried_in(): gathered = lax.all_gather(part, axis)]
    mul x10 -> x0, other arithmetic: 8.7 us -> none  [the longest x4 5.27 us: shards(): wetness * (lam + diffusion_step * neighbours(padded[1], couple_pad) - dam...]
    unnamed x30 -> x21, local copies, waits for them, and re-layouts: 3.65 us -> 9.59 us
    slice x16 -> x0, other arithmetic: 5.26 us -> none  [extended(): lax.slice_in_dim(block, block.shape[dim] - width, None, axis=dim)]
  transfers between devices with their start and end apart: 48 -> 0, of which waited for: 31 -> 0; matrix products, arithmetic and copies ran while one was open for 1% -> 0% of each run, Pallas kernels for 0% -> 0%
where the time goes in v1:
time: 50.9 us; the launch traced here: 50.4 us
  Pallas kernels  40.2 us (79%)
  local copies, waits for them, and re-layouts  9.59 us (19%)
  between operations  0.66 us (1%)
    pallas_call x1, Pallas kernels, shards(): pl.pallas_call(body, out_shape=(jax.ShapeDtypeStruct(direction.shape, f32...  40.2 us
    unnamed x21, local copies, waits for them, and re-layouts  9.59 us

profile of v1, /device:TPU:1, one launch (start us, length us, event | category | flops | bytes accessed | tf_op | source)
XLA Modules:
  0.0 50.4 jit_solution(13221201192991828333)
XLA Ops:
  0.6 0.0 copy-start
  0.6 1.3 %copy-done = f32[4,10,32,256]{3,2,1,0:T(8,128)S(1)} copy-done((f32[4,10,32,256]{3,2,1,0:T(8,128)S(1)}, f32[4,10,32,256]{3,2,1,0:T(8,128)}, u32[]{:S(2)}) %copy-start) | copy-done | bytes 1310744
  2.0 0.0 copy-start.1
  2.0 1.0 %copy-done.1 = f32[10,32,256]{2,1,0:T(8,128)S(1)} copy-done((f32[10,32,256]{2,1,0:T(8,128)S(1)}, f32[10,32,256]{2,1,0:T(8,128)}, u32[]{:S(2)}) %copy-start.1) | copy-done | bytes 327704
  2.9 0.0 copy-start.2
  2.9 1.0 %copy-done.2 = f32[10,32,256]{2,1,0:T(8,128)S(1)} copy-done((f32[10,32,256]{2,1,0:T(8,128)S(1)}, f32[10,32,256]{2,1,0:T(8,128)}, u32[]{:S(2)}) %copy-start.2) | copy-done | bytes 327704
  3.9 0.0 copy-start.3
  3.9 0.8 %copy-done.3 = s32[32,256]{1,0:T(8,128)S(1)} copy-done((s32[32,256]{1,0:T(8,128)S(1)}, s32[32,256]{1,0:T(8,128)}, u32[]{:S(2)}) %copy-start.3) | copy-done | bytes 32792
  4.7 0.0 copy-start.4
  4.7 0.8 %copy-done.4 = s32[32,256]{1,0:T(8,128)S(1)} copy-done((s32[32,256]{1,0:T(8,128)S(1)}, s32[32,256]{1,0:T(8,128)}, u32[]{:S(2)}) %copy-start.4) | copy-done | bytes 32792
  5.4 0.0 copy-start.5
  5.4 0.8 %copy-done.5 = s32[32,256]{1,0:T(8,128)S(1)} copy-done((s32[32,256]{1,0:T(8,128)S(1)}, s32[32,256]{1,0:T(8,128)}, u32[]{:S(2)}) %copy-start.5) | copy-done | bytes 32792
  6.2 0.0 copy-start.6
  6.2 0.7 %copy-done.6 = f32[20,32]{1,0:T(8,128)S(1)} copy-done((f32[20,32]{1,0:T(8,128)S(1)}, f32[20,32]{1,0:T(8,128)}, u32[]{:S(2)}) %copy-start.6) | copy-done | bytes 2584
  6.9 0.0 copy-start.7
  6.9 0.7 %copy-done.7 = f32[10]{0:T(128)S(1)} copy-done((f32[10]{0:T(128)S(1)}, f32[10]{0:T(128)}, u32[]{:S(2)}) %copy-start.7) | copy-done | bytes 64
  7.5 0.0 copy-start.8
  7.5 0.7 %copy-done.8 = f32[32]{0:T(128)S(1)} copy-done((f32[32]{0:T(128)S(1)}, f32[32]{0:T(128)}, u32[]{:S(2)}) %copy-start.8) | copy-done | bytes 152
  8.2 40.2 %shard_map.112 = (f32[10,32,256]{2,1,0:T(8,128)S(1)}, f32[10,32,256]{2,1,0:T(8,128)S(1)}, f32[10,32]{1,0:T(8,128)S(1)}) custom-call(f32[4,10,32,256]{3,2,1,0:T(8,128)S(1)} %copy-done, f32[10,32,256]{2,1,0:T(8,128)S(1)} %copy-done.1, f32[10,32,256]{2,1,0:T(8,128)S(1)} %copy-done.2, f32[10]{0:T(128)S(1)} %copy-done.7, f32[32]{0:T(128)S(1)} %copy-done.8, ...), custom_call_target="tpu_custom_call" | custom-call | flops 30000000 | bytes 3000000 | tf_op jit(solution)/shard_map/pallas_call | solution.py:384
  48.4 0.7 %copy.15 = f32[10,32,256]{2,1,0:T(8,128)} copy(f32[10,32,256]{2,1,0:T(8,128)S(1)} %get-tuple-element.6) | data formatting | bytes 655360
  49.1 0.7 %copy.16 = f32[10,32,256]{2,1,0:T(8,128)} copy(f32[10,32,256]{2,1,0:T(8,128)S(1)} %get-tuple-element.7) | data formatting | bytes 655360
  49.8 0.6 %copy.17 = f32[10,32]{1,0:T(8,128)} copy(f32[10,32]{1,0:T(8,128)S(1)} %get-tuple-element.8) | data formatting | bytes 2560
Async XLA Ops:
  0.6 1.3 %copy-start = (f32[4,10,32,256]{3,2,1,0:T(8,128)S(1)}, f32[4,10,32,256]{3,2,1,0:T(8,128)}, u32[]{:S(2)}) copy-start(f32[4,10,32,256]{3,2,1,0:T(8,128)} %states.1) | copy-start | bytes 3932164
  2.0 1.0 %copy-start.1 = (f32[10,32,256]{2,1,0:T(8,128)S(1)}, f32[10,32,256]{2,1,0:T(8,128)}, u32[]{:S(2)}) copy-start(f32[10,32,256]{2,1,0:T(8,128)} %direction.1) | copy-start | bytes 983044
  2.9 1.0 %copy-start.2 = (f32[10,32,256]{2,1,0:T(8,128)S(1)}, f32[10,32,256]{2,1,0:T(8,128)}, u32[]{:S(2)}) copy-start(f32[10,32,256]{2,1,0:T(8,128)} %mixing.1) | copy-start | bytes 983044
  3.9 0.8 %copy-start.3 = (s32[32,256]{1,0:T(8,128)S(1)}, s32[32,256]{1,0:T(8,128)}, u32[]{:S(2)}) copy-start(s32[32,256]{1,0:T(8,128)} %ocean.1) | copy-start | bytes 98308
  4.7 0.8 %copy-start.4 = (s32[32,256]{1,0:T(8,128)S(1)}, s32[32,256]{1,0:T(8,128)}, u32[]{:S(2)}) copy-start(s32[32,256]{1,0:T(8,128)} %atlantic.1) | copy-start | bytes 98308
  5.4 0.8 %copy-start.5 = (s32[32,256]{1,0:T(8,128)S(1)}, s32[32,256]{1,0:T(8,128)}, u32[]{:S(2)}) copy-start(s32[32,256]{1,0:T(8,128)} %levels_in.1) | copy-start | bytes 98308
  6.2 0.7 %copy-start.6 = (f32[20,32]{1,0:T(8,128)S(1)}, f32[20,32]{1,0:T(8,128)}, u32[]{:S(2)}) copy-start(f32[20,32]{1,0:T(8,128)} %cost_weight.1) | copy-start | bytes 7684
  6.9 0.7 %copy-start.7 = (f32[10]{0:T(128)S(1)}, f32[10]{0:T(128)}, u32[]{:S(2)}) copy-start(f32[10]{0:T(128)} %level_dz.1) | copy-start | bytes 124
  7.5 0.7 %copy-start.8 = (f32[32]{0:T(128)S(1)}, f32[32]{0:T(128)}, u32[]{:S(2)}) copy-start(f32[32]{0:T(128)} %lat_width.1) | copy-start | bytes 388

commit v2 on v1

v2 whole, which is shorter than its diff:
```python
import functools
import math

import jax
import jax.numpy as jnp
from jax import lax
from jax.experimental import pallas as pl
from jax.experimental.pallas import tpu as pltpu
from jax.sharding import PartitionSpec as P

MESH = pl.DeviceIdType.MESH
diffusion_step = 0.08
cubic_drag = 0.15

HALO = 4
LINE = 4


def around(couple, value, level, part, here=None):
    if here is None:
        here = couple[level] if value is None else couple[level] * value[level]
    rows, columns = here.shape
    total = pltpu.roll(here, 1, 1) + pltpu.roll(here, columns - 1, 1)
    total = (total + (pltpu.roll(here, 1, 0) + pltpu.roll(here, rows - 1, 0)))[part]
    for k in (level - 1, level + 1):
        if k >= 0:
            there = couple[(k,) + part]
            total = total + (there if value is None else there * value[(k,) + part])
    return total


def kernel(
    n_lon, n_lat, n_depth, scale, grid_scale,
    states, direction, mixing, dz_in_hbm, width_in_hbm, weight_in_hbm, ocean, atlantic, levels_in,
    hess, grad, overturning,
    st_states, st_dir, st_mix, st_ocean, st_atl, st_lev, cost_weight, level_dz, lat_width,
    fields, capacity, tan1, tan2, tan3, tan3_wide, lam, mu,
    flat, edges, rows_out, rows_in, strips_out, strips_in, strip3_out, strip3_in, dz_out, dz_in, zone, zones, totals, prefixes, weights,
    in_sem, lat_send, lat_recv, lon_send, lon_recv, dep_send, dep_recv, zone_send, zone_recv, ready,
):
    layers, rows, columns = direction.shape
    all_layers = 2 * layers
    ext_rows, ext_columns = fields.shape[-2:]
    lon, lat, dep = lax.axis_index("lon"), lax.axis_index("lat"), lax.axis_index("depth")
    wrap = lambda value, size: lax.rem(value + size, size)

    def at(dl=0, dz=0, dd=0):
        return (wrap(lon + dl, n_lon), wrap(lat + dz, n_lat), wrap(dep + dd, n_depth))

    plane = [(i, d) for d in range(n_depth) for i in range(n_lon) if i or d]
    start = lon // LINE * LINE
    across = [at(dl=LINE * i) for i in range(1, n_lon // LINE)]
    peers = [
        (start + lax.rem(lon - start + i, LINE), lat, wrap(dep + d, n_depth))
        for d in range(n_depth) for i in range(LINE) if i or d
    ]
    peers += across + [at(dl=i) for i in (1, -1)] + [at(dz=z) for z in (1, -1)]
    barrier = pltpu.get_barrier_semaphore()
    for peer in peers:
        pl.semaphore_signal(barrier, inc=1, device_id=peer, device_id_type=MESH)

    loads = [
        pltpu.make_async_copy(src, dst, in_sem.at[i])
        for i, (src, dst) in enumerate((
            (width_in_hbm, lat_width), (weight_in_hbm, cost_weight), (dz_in_hbm, level_dz), (levels_in, st_lev),
            (ocean, st_ocean), (atlantic, st_atl), (mixing, st_mix), (direction, st_dir), (states, st_states),
        ))
    ]
    for load in loads:
        load.start()

    sends, expected = [], {}

    def send(src, dst, send_sem, recv_sem, device):
        copy = pltpu.make_async_remote_copy(
            src_ref=src, dst_ref=dst, send_sem=send_sem, recv_sem=recv_sem, device_id=device, device_id_type=MESH
        )
        copy.start()
        sends.append(copy)
        expected[id(copy)] = copy
        return copy

    def arrive(*copies):
        for copy in copies:
            expected.pop(id(copy)).wait_recv()

    def finish():
        for copy in list(expected.values()):
            arrive(copy)
        for copy in sends:
            copy.wait_send()

    upright = dep == 0
    own = lambda j: jnp.where(upright, j, layers - 1 - j)
    lane = lax.broadcasted_iota(jnp.int32, (rows, 128), 1)
    group = lane // HALO
    row = lax.broadcasted_iota(jnp.int32, (rows, 128), 0)

    for load in loads[:3]:
        load.wait()
    width = jnp.zeros((rows, 128), jnp.float32)
    for r in range(rows):
        width = jnp.where(row == r, lat_width[r], width)
    square_row = lax.broadcasted_iota(jnp.int32, (rows, rows), 0)
    square_lane = lax.broadcasted_iota(jnp.int32, (rows, rows), 1)
    by_level = jnp.zeros((rows, 128), jnp.float32)
    for k in range(all_layers):
        line = cost_weight[pl.ds(jnp.where(upright, k, all_layers - 1 - k), 1), :]
        column = jnp.sum(jnp.where(square_row == square_lane, line, 0.0), axis=1, keepdims=True)
        by_level = jnp.where(lane == k, column * grid_scale, by_level)
    flat[0:rows, 0:128] = by_level
    dz_out[...] = jnp.zeros(dz_out.shape, jnp.float32) + level_dz[own(layers - 1)] * scale

    for load in loads[3:]:
        load.wait()
    basin = st_atl[...].astype(jnp.float32) * jnp.concatenate([width] * (columns // 128), axis=1)
    flat[0:rows, 128 : 128 + columns] = basin
    reach = st_lev[...] * st_ocean[...]

    edge = columns - 128
    packed = [[jnp.zeros((rows, 128), jnp.float32)] * 2 for _ in range(2)]

    def pack(pair, block, slot):
        right = pltpu.roll(block[:, edge:], (HALO * slot) % 128, 1)
        left = pltpu.roll(block[:, :128], (HALO * slot) % 128, 1)
        pair[0] = jnp.where(group == (slot - 1) % 32, right, pair[0])
        pair[1] = jnp.where(group == slot, left, pair[1])

    pack(packed[0], basin, 3 * layers)
    upper = lax.broadcasted_iota(jnp.int32, (2 * HALO, columns), 0) < HALO
    held = None
    for j in range(layers):
        k = own(j)
        wet = dep * layers + k < reach
        couple = jnp.where(wet, math.sqrt(diffusion_step) * st_mix[k], 0.0)
        parts = [couple, st_dir[k]]
        parts += [jnp.where(wet, math.sqrt(3.0 * cubic_drag) * st_states[s, k], 0.0) for s in range(4)]
        for f, part in enumerate(parts):
            fields[f, j, 0:rows, 0:columns] = part
            pack(packed[f // 3], part, (f % 3) * layers + j)
            if f < 3 and j % 2:
                before, after = held[f][0 : 2 * HALO], pltpu.roll(part[0 : 2 * HALO], HALO, 0)
                rows_out[0, f, j // 2] = jnp.where(upper, before, after)
                before, after = held[f][rows - 2 * HALO :], pltpu.roll(part[rows - 2 * HALO :], HALO, 0)
                rows_out[1, f, j // 2] = jnp.where(upper, after, before)
        held = parts
    for m in range(2):
        for way in range(2):
            strips_out[m, way] = packed[m][way]

    pl.semaphore_wait(barrier, len(peers))
    for peer in across:
        pl.semaphore_signal(ready, inc=1, device_id=peer, device_id_type=MESH)

    every = slice(0, layers)
    inner = (slice(0, rows), slice(0, columns))
    bottom = (slice(rows, ext_rows), slice(0, ext_columns))
    side = (slice(0, rows), slice(columns, ext_columns))
    frame = (bottom, side)
    whole = (slice(0, ext_rows), slice(0, ext_columns))
    bottom_level = layers - 1

    def send_rows(ref, lead, lanes, i, first=0, last=HALO):
        near, below = slice(first, last), slice(rows + first, rows + last)
        far, above = slice(rows - last, rows - first), slice(ext_rows - last, ext_rows - first)
        return [
            send(ref.at[lead + (src, lanes)], ref.at[lead + (dst, lanes)], lat_send.at[2 * i + n], lat_recv.at[2 * i + n], at(dz=dz))
            for n, (src, dst, dz) in enumerate(((near, below, -1), (far, above, 1)))
        ]

    def send_strips(out, into, i):
        return [
            send(out.at[way], into.at[way, 0:rows], lon_send.at[2 * i + way], lon_recv.at[2 * i + way], at(dl=dl))
            for way, dl in ((0, 1), (1, -1))
        ]

    def send_part(src, dst, i):
        return send(src, dst, dep_send.at[i], dep_recv.at[i], at(dd=1))

    def send_level(ref, i):
        return send_part(ref.at[bottom_level], ref.at[layers], i)

    strips = send_strips(strips_out.at[0], strips_in.at[0], 0)
    first_rows = [
        send(rows_out.at[i], rows_in.at[i], lat_send.at[i], lat_recv.at[i], at(dz=dz)) for i, dz in ((0, -1), (1, 1))
    ]
    strips += send_strips(strips_out.at[1], strips_in.at[1], 1)
    last_rows = [
        send(
            fields.at[5, every, pl.ds(src, 1), inner[1]], edges.at[every, pl.ds(dst, 1), inner[1]],
            lat_send.at[2 + i], lat_recv.at[2 + i], at(dz=dz),
        )
        for i, (src, dst, dz) in enumerate(((0, 0, -1), (rows - 1, 2 * HALO - 1, 1)))
    ]
    first_level = [
        send_part(fields.at[(slice(0, 2), bottom_level) + inner], fields.at[(slice(0, 2), layers) + inner], 0),
        send_part(fields.at[(5, bottom_level) + inner], fields.at[(5, layers) + inner], 1),
        send_part(dz_out, dz_in, 2),
    ]

    arrive(*strips)
    corners = send_rows(strips_in, (slice(0, 2), slice(0, 2)), slice(0, 128), 2)
    drag_rows = [
        send_rows(fields, (3, every), inner[1], 3, 0, 2),
        send_rows(fields, (4, every), inner[1], 4, 0, 2),
    ]
    flat_rows = send_rows(flat, (), slice(0, 128 + columns), 6)

    lane_x = lax.broadcasted_iota(jnp.int32, (ext_rows, 128), 1)
    even = (lane_x // HALO) % 2 == 0

    def combine(pair, part):
        from_left, from_right = pair[0, part], pair[1, part]
        return [jnp.where(even[part], from_right, from_left), jnp.where(even[part], from_left, from_right)]

    def unpack(both, slot):
        return pltpu.roll(both[slot % 2], (128 - HALO * slot) % 128, 1)

    one = lambda flag: jnp.where(flag, 1.0, 0.0).astype(jnp.float32)
    lane_mask = jnp.where(lane_x < HALO, one(lon < n_lon - 1), jnp.where(lane_x >= 128 - HALO, one(lon > 0), 0.0))
    row_8 = lax.broadcasted_iota(jnp.int32, (2 * HALO, ext_columns), 0)
    row_mask = jnp.where(row_8 < HALO, one(lat < n_lat - 1), one(lat > 0))
    couple = fields.at[0]

    def unpack_all(part):
        for m in range(2):
            both = combine(strips_in.at[m], part)
            for f in range(3):
                for j in range(layers):
                    halo = unpack(both, f * layers + j)
                    if m == 0 and f == 0:
                        halo = halo * lane_mask[part]
                        if part.start:
                            halo = halo * row_mask[:, columns:]
                    fields[3 * m + f, j, part, columns:] = halo
            if m == 0:
                flat[part, 128 + columns :] = unpack(both, 3 * layers)

    unpack_all(slice(0, rows))
    arrive(*first_rows)
    for f in range(3):
        for pair in range(layers // 2):
            from_next, from_previous = rows_in[0, f, pair], rows_in[1, f, pair]
            both = [
                jnp.where(upper, from_next, from_previous),
                pltpu.roll(jnp.where(upper, from_previous, from_next), HALO, 0),
            ]
            for odd in range(2):
                halo = both[odd] if f else both[odd] * row_mask[:, 0:columns]
                fields[f, 2 * pair + odd, rows:, 0:columns] = halo
    arrive(*last_rows)
    arrive(*first_level)

    tangents = [fields.at[1], tan1, tan2, tan3]
    drag = [fields.at[2 + s] for s in range(4)]

    def capacity_at(j, part):
        here = couple[(j,) + part]
        capacity[(j,) + part] = jnp.where(here > 0.0, 1.0, 0.0) - here * around(couple, None, j, part)

    def tangent_at(s, j, part):
        value = tangents[s]
        at_part = (j,) + part
        damp = drag[s][at_part]
        return couple[at_part] * around(couple, value, j, part) + (capacity[at_part] - damp * damp) * value[at_part]

    def zonal(block, j):
        weighted = block * flat[0:rows, 128 : 128 + columns]
        folded = weighted[:, 0:128]
        for part in range(1, columns // 128):
            folded = folded + weighted[:, 128 * part : 128 * part + 128]
        return jnp.sum(folded, axis=1, keepdims=True) * (level_dz[own(j)] * scale)

    tiles = rows // 8
    lane_8 = lax.broadcasted_iota(jnp.int32, (8, 128), 1)

    def put(sums, column, j):
        for t in range(tiles):
            sums = jnp.where(lane_8 == t * layers + j, column[8 * t : 8 * t + 8], sums)
        return sums

    def gather(f, sums):
        zone[f] = sums
        zones[f, lon] = sums
        return [
            send(zone.at[f], zones.at[f, lon + (n_lon if dd else 0)], zone_send.at[f, i], zone_recv.at[f, i], at(dl=dl, dd=dd))
            for i, (dl, dd) in enumerate(plane)
        ]

    last = drag[3]
    sums = jnp.zeros((8, 128), jnp.float32)
    for j in range(layers):
        capacity_at(j, inner)
    for j in range(layers):
        here = last[(j,) + inner]
        outer = jnp.concatenate([edges[j], jnp.zeros((2 * HALO, ext_columns - columns), jnp.float32)], axis=1)
        spread = jnp.concatenate([couple[j, 0:rows] * last[j, 0:rows], couple[j, rows:] * outer], axis=0)
        final = couple[(j,) + inner] * around(couple, last, j, inner, spread)
        final = final + (capacity[(j,) + inner] - here * here * (1.0 / 3.0)) * here
        sums = put(sums, zonal(final, j) * (1.0 / math.sqrt(3.0 * cubic_drag)), j)
    pl.semaphore_wait(ready, len(across))
    gathered_0 = gather(0, sums)
    drag_rows.append(send_rows(fields, (5, every), inner[1], 5, 0, 3))
    for j in range(layers):
        tan1[(j,) + inner] = tangent_at(0, j, inner)

    arrive(*corners)
    unpack_all(slice(rows, ext_rows))
    border = [
        send_part(fields.at[(slice(0, 2), bottom_level) + part], fields.at[(slice(0, 2), layers) + part], 3 + i)
        for i, part in enumerate(frame)
    ]
    for j in range(layers):
        if j == bottom_level:
            arrive(*border)
        for part in frame:
            capacity_at(j, part)
            tan1[(j,) + part] = tangent_at(0, j, part)
    pending = send_level(tan1, 5)

    for s in (1, 2):
        nxt = tangents[s + 1]
        arrive(*drag_rows[s - 1])
        for j in range(layers):
            if j == bottom_level:
                arrive(pending)
            nxt[j] = tangent_at(s, j, whole)
        pending = send_level(nxt, 5 + s)

    pair = [jnp.zeros((rows, 128), jnp.float32)] * 2
    for j in range(layers):
        block = tan3[(j,) + inner]
        tan3_wide[(j,) + inner] = block
        pack(pair, block, j)
    strip3_out[0] = pair[0]
    strip3_out[1] = pair[1]
    strips = send_strips(strip3_out, strip3_in, 2)
    third_rows = send_rows(tan3_wide, (every,), inner[1], 7)

    sums = jnp.zeros((8, 128), jnp.float32)
    for j in range(layers):
        if j == bottom_level:
            arrive(pending)
        sums = put(sums, zonal(tangent_at(3, j, inner), j), j)
    gathered_1 = gather(1, sums)

    def collect(f):
        mine = zones[f, 0]
        other = zones[f, n_lon]
        for i in range(1, n_lon):
            mine = mine + zones[f, i]
            other = other + zones[f, n_lon + i]
        for t in range(tiles):
            shift = (128 - layers * t) % 128
            a = pltpu.roll(mine, shift, 1) if shift else mine
            b = pltpu.roll(other, (shift + layers) % 128, 1)
            totals[f, 8 * t : 8 * t + 8] = jnp.where(lane_8 < layers, a, b)
        return send_rows(totals, (f,), slice(0, 128), 8 + f)

    def prefix_rows(f, part):
        count = part.stop - part.start
        places = [k if k < layers else layers + all_layers - 1 - k for k in range(all_layers)]
        terms = [jnp.broadcast_to(totals[f, part, p : p + 1], (count, 128)) for p in places]
        stream = both_ways(terms, upright, False)
        prefix = both_ways([weights[k, part] * stream[k] for k in range(all_layers)], upright, True)
        for k in range(layers + 1):
            prefixes[f, k, part] = prefix[k]
        return stream

    arrive(*flat_rows, *drag_rows[2])
    for k in range(all_layers):
        weights[k] = jnp.broadcast_to(flat[:, k : k + 1], (ext_rows, 128))

    def start_adjoint(f, ref):
        basin = flat[:, 128:]
        for j in range(layers + 1):
            thick = level_dz[own(j)] * scale if j < layers else dz_in[0:1, 0:1]
            ref[0, j] = basin * thick * jnp.concatenate([prefixes[f, j]] * (ext_columns // 128), axis=1)

    def adjoint_at(ref, n, j, part):
        at_part = (j,) + part
        damp = drag[3 - n][at_part]
        keep = capacity[at_part] - damp * damp
        return couple[at_part] * around(couple, ref.at[n], j, part) + keep * ref[(n,) + at_part], damp

    def lam_step(n, waits):
        for j in range(layers):
            if j == bottom_level:
                arrive(*waits)
            if n < 3:
                lam[n + 1, j] = adjoint_at(lam, n, j, whole)[0]
            else:
                grad[own(j)] = adjoint_at(lam, n, j, inner)[0]
        return [send_level(lam.at[n + 1], 8 + n)] if n < 3 else []

    ratio = 6.0 * cubic_drag / math.sqrt(3.0 * cubic_drag)

    def mu_step(n, waits):
        part = whole if n < 3 else inner
        tangent = tan3_wide if n == 0 else tangents[3 - n]
        for j in range(layers):
            if j == bottom_level:
                arrive(*waits)
            new, damp = adjoint_at(mu, n, j, part)
            new = new - (ratio * damp) * (tangent[(j,) + part] * lam[(n, j) + part])
            if n < 3:
                mu[n + 1, j] = new
            else:
                hess[own(j)] = new
        return [send_level(mu.at[n + 1], 11 + n)] if n < 3 else []

    arrive(*gathered_0)
    border = collect(0)
    streams = prefix_rows(0, slice(0, rows))
    spots = lax.broadcasted_iota(jnp.int32, (rows, rows), 0) == lax.broadcasted_iota(jnp.int32, (rows, rows), 1)
    for j in range(layers):
        line = jnp.sum(jnp.where(spots, streams[j][:, 0:rows], 0.0), axis=0, keepdims=True)
        overturning[pl.ds(own(j), 1), :] = line
    arrive(*strips)
    corners = send_rows(strip3_in, (slice(0, 2),), slice(0, 128), 10)
    arrive(*border)
    prefix_rows(0, slice(rows, ext_rows))
    start_adjoint(0, lam)
    pending = lam_step(0, [])
    pending = lam_step(1, pending)

    arrive(*gathered_1)
    border = collect(1)
    prefix_rows(1, slice(0, rows))
    arrive(*third_rows, *corners)
    both = combine(strip3_in, slice(0, ext_rows))
    for j in range(layers):
        tan3_wide[j, :, columns:] = unpack(both, j)
    pending = lam_step(2, pending)
    lam_step(3, pending)

    arrive(*border)
    prefix_rows(1, slice(rows, ext_rows))
    start_adjoint(1, mu)
    pending = []
    for n in range(4):
        pending = mu_step(n, pending)
    finish()


def both_ways(terms, upright, forward):
    count = len(terms)
    up = [terms[0]]
    for k in range(1, count):
        up.append(up[-1] + terms[k])
    down = [terms[-1]]
    for k in range(count - 2, -1, -1):
        down.append(down[-1] + terms[k])
    down = down[::-1]
    choose_up = upright if forward else jnp.logical_not(upright)
    return [jnp.where(choose_up, a, b) for a, b in zip(up, down)]


def store(hess, grad, overturning, hess_out, grad_out, overturning_out, sem):
    copies = [
        pltpu.make_async_copy(src, dst, sem.at[i])
        for i, (src, dst) in enumerate(((hess, hess_out), (grad, grad_out), (overturning, overturning_out)))
    ]
    for copy in copies:
        copy.start()
    for copy in copies:
        copy.wait()


def solution(mesh):
    n_lon, n_lat, n_depth = (mesh.shape[name] for name in ("lon", "lat", "depth"))

    def shards(states, direction, mixing, level_dz, lat_width, cost_weight, ocean_columns, atlantic, levels):
        layers, rows, columns = direction.shape
        ext = (rows + 2 * HALO, columns + 128)
        tall = (layers + 1,) + ext
        f32, i32 = jnp.float32, jnp.int32
        vmem = lambda *shape: pltpu.VMEM(shape, f32)
        dma = lambda count: pltpu.SemaphoreType.DMA((count,))
        in_vmem, in_hbm = (pl.BlockSpec(memory_space=m) for m in (pltpu.VMEM, pltpu.HBM))
        scale = 1.0 / math.sqrt(columns * n_lon * layers * n_depth)
        body = functools.partial(kernel, n_lon, n_lat, n_depth, scale, math.sqrt(columns * n_lon))
        results = pl.pallas_call(
            body,
            out_shape=(vmem(*direction.shape), vmem(*direction.shape), vmem(layers, rows)),
            in_specs=[in_hbm] * 9,
            out_specs=(in_vmem,) * 3,
            scratch_shapes=[
                vmem(*states.shape), vmem(*direction.shape), vmem(*direction.shape),
                pltpu.VMEM((rows, columns), i32), pltpu.VMEM((rows, columns), i32), pltpu.VMEM((rows, columns), i32),
                vmem(*cost_weight.shape), pltpu.SMEM(level_dz.shape, f32), pltpu.SMEM(lat_width.shape, f32),
                vmem(6, *tall), vmem(layers, *ext), vmem(*tall), vmem(*tall), vmem(*tall),
                vmem(layers, *ext), vmem(4, *tall), vmem(4, *tall),
                vmem(ext[0], 128 + ext[1]), vmem(layers, 2 * HALO, columns),
                vmem(2, 3, layers // 2, 2 * HALO, columns), vmem(2, 3, layers // 2, 2 * HALO, columns),
                vmem(2, 2, rows, 128), vmem(2, 2, ext[0], 128),
                vmem(2, rows, 128), vmem(2, ext[0], 128), vmem(8, 128), vmem(8, 128),
                vmem(2, 8, 128), vmem(2, 2 * n_lon, 8, 128), vmem(2, ext[0], 128),
                vmem(2, layers + 1, ext[0], 128), vmem(n_depth * layers, ext[0], 128),
                dma(9), dma(22), dma(22), dma(6), dma(6), dma(14), dma(14),
                pltpu.SemaphoreType.DMA((2, 2 * n_lon - 1)), pltpu.SemaphoreType.DMA((2, 2 * n_lon - 1)),
                pltpu.SemaphoreType.REGULAR,
            ],
            compiler_params=pltpu.CompilerParams(
                collective_id=0, has_side_effects=True, vmem_limit_bytes=48 * 2**20
            ),
            cost_estimate=pl.CostEstimate(flops=3 * 10**7, bytes_accessed=3 * 10**6, transcendentals=0),
        )(*(
            pltpu.with_memory_space_constraint(x, pltpu.HBM)
            for x in (states, direction, mixing, level_dz, lat_width, cost_weight, ocean_columns, atlantic, levels)
        ))
        return pl.pallas_call(
            store,
            out_shape=tuple(jax.ShapeDtypeStruct(result.shape, f32) for result in results),
            in_specs=[in_vmem] * 3,
            out_specs=(in_hbm,) * 3,
            scratch_shapes=[dma(3)],
            cost_estimate=pl.CostEstimate(flops=0, bytes_accessed=10**6, transcendentals=0),
        )(*(pltpu.with_memory_space_constraint(result, pltpu.VMEM) for result in results))

    placed = (
        P(None, "depth", "lat", "lon"),
        P("depth", "lat", "lon"),
        P("depth", "lat", "lon"),
        P("depth"),
        P("lat"),
        P(None, "lat"),
        P("lat", "lon"),
        P("lat", "lon"),
        P("lat", "lon"),
    )
    return jax.shard_map(
        shards,
        mesh=mesh,
        in_specs=placed,
        out_specs=(P("depth", "lat", "lon"), P("depth", "lat", "lon"), P("depth", "lat")),
        check_vma=False,
    )
```

time: 50.9 us -> 38.7 us (0.76)
  local copies, waits for them, and re-layouts: 9.59 us -> 0 us
  Pallas kernels: 40.2 us -> 38 us
    unnamed x21 -> x0, local copies, waits for them, and re-layouts: 9.59 us -> none
    pallas_call x1 -> x2, Pallas kernels: 40.2 us -> 38 us  [the longest x1 37.1 us: shards(): pl.pallas_call(body, out_shape=(vmem(*direction.shape), vmem(*direction.s...]
where the time goes in v2:
time: 38.7 us; the launch traced here: 38.6 us
  Pallas kernels  38 us (98%)
  between operations  0.64 us (2%)
    pallas_call x1, Pallas kernels, shards(): pl.pallas_call(body, out_shape=(vmem(*direction.shape), vmem(*direction.s...  37.1 us
    pallas_call x1, Pallas kernels, shards(): pl.pallas_call(store, out_shape=tuple((jax.ShapeDtypeStruct(result.shape,...  0.86 us

profile of v2, /device:TPU:1, one launch (start us, length us, event | category | flops | bytes accessed | tf_op | source)
XLA Modules:
  0.0 38.6 jit_solution(18163213051374790127)
XLA Ops:
  0.6 37.1 %shard_map.112 = (f32[10,32,256]{2,1,0:T(8,128)S(1)}, f32[10,32,256]{2,1,0:T(8,128)S(1)}, f32[10,32]{1,0:T(8,128)S(1)}) custom-call(f32[4,10,32,256]{3,2,1,0:T(8,128)} %states.1, f32[10,32,256]{2,1,0:T(8,128)} %direction.1, f32[10,32,256]{2,1,0:T(8,128)} %mixing.1, f32[10]{0:T(128)} %dz_in_hbm.1, f32[32]{0:T(128)} %width_in_hbm.1, f32[20,32]{1,0:T(8,128)} %weight_in_hbm.1, ...), custom_call_target="tpu_custom_call" | custom-call | flops 30000000 | bytes 3000000 | tf_op jit(solution)/shard_map/pallas_call | solution.py:483
  37.7 0.9 %shard_map.113 = (f32[10,32,256]{2,1,0:T(8,128)}, f32[10,32,256]{2,1,0:T(8,128)}, f32[10,32]{1,0:T(8,128)}) custom-call(f32[10,32,256]{2,1,0:T(8,128)S(1)} %get-tuple-element.6.hess, f32[10,32,256]{2,1,0:T(8,128)S(1)} %get-tuple-element.7.grad, f32[10,32]{1,0:T(8,128)S(1)} %get-tuple-element.8.overturning), custom_call_target="tpu_custom_call" | custom-call | bytes 1000000 | tf_op jit(solution)/shard_map/pallas_call | solution.py:512

commit v3 on v2

--- a/solution.py
+++ b/solution.py
@@ -1,4 +1,5 @@
 import functools
+import itertools
 import math
 
 import jax
@@ -14,6 +15,7 @@
 
 HALO = 4
 LINE = 4
+DEEP = 4
 
 
 def around(couple, value, level, part, here=None):
@@ -109,7 +111,10 @@
         column = jnp.sum(jnp.where(square_row == square_lane, line, 0.0), axis=1, keepdims=True)
         by_level = jnp.where(lane == k, column * grid_scale, by_level)
     flat[0:rows, 0:128] = by_level
-    dz_out[...] = jnp.zeros(dz_out.shape, jnp.float32) + level_dz[own(layers - 1)] * scale
+    thick = jnp.zeros(dz_out.shape, jnp.float32)
+    for i in range(DEEP):
+        thick = jnp.where(lax.broadcasted_iota(jnp.int32, dz_out.shape, 0) == i, level_dz[own(layers - 1 - i)] * scale, thick)
+    dz_out[...] = thick
 
     for load in loads[3:]:
         load.wait()
@@ -174,11 +179,17 @@
             for way, dl in ((0, 1), (1, -1))
         ]
 
-    def send_part(src, dst, i):
+    parts_sent = itertools.count()
+
+    def send_part(src, dst):
+        i = next(parts_sent)
         return send(src, dst, dep_send.at[i], dep_recv.at[i], at(dd=1))
 
-    def send_level(ref, i):
-        return send_part(ref.at[bottom_level], ref.at[layers], i)
+    def send_deep(ref, i, part):
+        return send_part(ref.at[(bottom_level - i,) + part], ref.at[(layers + i,) + part])
+
+    def send_level(ref):
+        return send_deep(ref, 0, whole)
 
     strips = send_strips(strips_out.at[0], strips_in.at[0], 0)
     first_rows = [
@@ -193,9 +204,9 @@
         for i, (src, dst, dz) in enumerate(((0, 0, -1), (rows - 1, 2 * HALO - 1, 1)))
     ]
     first_level = [
-        send_part(fields.at[(slice(0, 2), bottom_level) + inner], fields.at[(slice(0, 2), layers) + inner], 0),
-        send_part(fields.at[(5, bottom_level) + inner], fields.at[(5, layers) + inner], 1),
-        send_part(dz_out, dz_in, 2),
+        send_part(fields.at[(slice(0, 2), bottom_level) + inner], fields.at[(slice(0, 2), layers) + inner]),
+        send_part(fields.at[(5, bottom_level) + inner], fields.at[(5, layers) + inner]),
+        send_part(dz_out, dz_in),
     ]
 
     arrive(*strips)
@@ -307,8 +318,8 @@
     arrive(*corners)
     unpack_all(slice(rows, ext_rows))
     border = [
-        send_part(fields.at[(slice(0, 2), bottom_level) + part], fields.at[(slice(0, 2), layers) + part], 3 + i)
-        for i, part in enumerate(frame)
+        send_part(fields.at[(slice(0, 2), bottom_level) + part], fields.at[(slice(0, 2), layers) + part])
+        for part in frame
     ]
     for j in range(layers):
         if j == bottom_level:
@@ -316,7 +327,7 @@
         for part in frame:
             capacity_at(j, part)
             tan1[(j,) + part] = tangent_at(0, j, part)
-    pending = send_level(tan1, 5)
+    pending = send_level(tan1)
 
     for s in (1, 2):
         nxt = tangents[s + 1]
@@ -325,7 +336,7 @@
             if j == bottom_level:
                 arrive(pending)
             nxt[j] = tangent_at(s, j, whole)
-        pending = send_level(nxt, 5 + s)
+        pending = send_level(nxt)
 
     pair = [jnp.zeros((rows, 128), jnp.float32)] * 2
     for j in range(layers):
@@ -363,19 +374,24 @@
         terms = [jnp.broadcast_to(totals[f, part, p : p + 1], (count, 128)) for p in places]
         stream = both_ways(terms, upright, False)
         prefix = both_ways([weights[k, part] * stream[k] for k in range(all_layers)], upright, True)
-        for k in range(layers + 1):
+        for k in range(layers + DEEP):
             prefixes[f, k, part] = prefix[k]
         return stream
 
     arrive(*flat_rows, *drag_rows[2])
+    deep = [send_deep(couple, i, whole) for i in range(1, DEEP)]
+    deep += [send_deep(drag[3], 0, part) for part in frame]
+    deep += [send_deep(drag[s], i, whole) for s, i in ((3, 1), (3, 2), (2, 0), (2, 1), (1, 0))]
+    deep += [send_deep(tan2, 1, whole)]
+    deep_third = [send_deep(tan3_wide, i, inner) for i in range(3)]
     for k in range(all_layers):
         weights[k] = jnp.broadcast_to(flat[:, k : k + 1], (ext_rows, 128))
 
-    def start_adjoint(f, ref):
-        basin = flat[:, 128:]
-        for j in range(layers + 1):
-            thick = level_dz[own(j)] * scale if j < layers else dz_in[0:1, 0:1]
-            ref[0, j] = basin * thick * jnp.concatenate([prefixes[f, j]] * (ext_columns // 128), axis=1)
+    def start_adjoint(f, ref, part):
+        basin = flat[part, 128:]
+        for j in range(layers + DEEP):
+            thick = level_dz[own(j)] * scale if j < layers else dz_in[j - layers : j - layers + 1, 0:1]
+            ref[0, j, part] = basin * thick * jnp.concatenate([prefixes[f, j, part]] * (ext_columns // 128), axis=1)
 
     def adjoint_at(ref, n, j, part):
         at_part = (j,) + part
@@ -383,63 +399,73 @@
         keep = capacity[at_part] - damp * damp
         return couple[at_part] * around(couple, ref.at[n], j, part) + keep * ref[(n,) + at_part], damp
 
-    def lam_step(n, waits):
-        for j in range(layers):
-            if j == bottom_level:
-                arrive(*waits)
+    def lam_step(n):
+        for j in range(layers + 3 - n):
             if n < 3:
                 lam[n + 1, j] = adjoint_at(lam, n, j, whole)[0]
             else:
                 grad[own(j)] = adjoint_at(lam, n, j, inner)[0]
-        return [send_level(lam.at[n + 1], 8 + n)] if n < 3 else []
 
     ratio = 6.0 * cubic_drag / math.sqrt(3.0 * cubic_drag)
 
-    def mu_step(n, waits):
-        part = whole if n < 3 else inner
+    def mu_step(n, bands):
         tangent = tan3_wide if n == 0 else tangents[3 - n]
-        for j in range(layers):
-            if j == bottom_level:
-                arrive(*waits)
-            new, damp = adjoint_at(mu, n, j, part)
-            new = new - (ratio * damp) * (tangent[(j,) + part] * lam[(n, j) + part])
-            if n < 3:
-                mu[n + 1, j] = new
-            else:
-                hess[own(j)] = new
-        return [send_level(mu.at[n + 1], 11 + n)] if n < 3 else []
+        for j in range(layers + 3 - n):
+            for band in bands:
+                part = (band, whole[1] if n < 3 else inner[1])
+                new, damp = adjoint_at(mu, n, j, part)
+                new = new - (ratio * damp) * (tangent[(j,) + part] * lam[(n, j) + part])
+                if n < 3:
+                    mu[(n + 1, j) + part] = new
+                else:
+                    hess[(own(j),) + part] = new
 
     arrive(*gathered_0)
     border = collect(0)
-    streams = prefix_rows(0, slice(0, rows))
+    streams = prefix_rows(0, inner[0])
     spots = lax.broadcasted_iota(jnp.int32, (rows, rows), 0) == lax.broadcasted_iota(jnp.int32, (rows, rows), 1)
     for j in range(layers):
         line = jnp.sum(jnp.where(spots, streams[j][:, 0:rows], 0.0), axis=0, keepdims=True)
         overturning[pl.ds(own(j), 1), :] = line
     arrive(*strips)
     corners = send_rows(strip3_in, (slice(0, 2),), slice(0, 128), 10)
+    both = combine(strip3_in, inner[0])
+    for j in range(layers):
+        tan3_wide[(j,) + side] = unpack(both, j)
+    deep_third += [send_deep(tan3_wide, i, side) for i in range(3)]
+    arrive(*deep)
+    for j in range(layers, layers + 3):
+        capacity_at(j, whole)
+    start_adjoint(0, lam, inner[0])
     arrive(*border)
-    prefix_rows(0, slice(rows, ext_rows))
-    start_adjoint(0, lam)
-    pending = lam_step(0, [])
-    pending = lam_step(1, pending)
+    prefix_rows(0, bottom[0])
+    start_adjoint(0, lam, bottom[0])
+    lam_step(0)
+    lam_step(1)
 
     arrive(*gathered_1)
     border = collect(1)
-    prefix_rows(1, slice(0, rows))
+    prefix_rows(1, inner[0])
+    start_adjoint(1, mu, inner[0])
+    arrive(*deep_third)
+    lam_step(2)
+    for n in range(3):
+        mu_step(n, [inner[0]])
+    mu_step(3, [slice(8, rows - 8)])
     arrive(*third_rows, *corners)
-    both = combine(strip3_in, slice(0, ext_rows))
-    for j in range(layers):
-        tan3_wide[j, :, columns:] = unpack(both, j)
-    pending = lam_step(2, pending)
-    lam_step(3, pending)
+    both = combine(strip3_in, bottom[0])
+    for j in range(layers):
+        tan3_wide[j, bottom[0], columns:] = unpack(both, j)
+    deep_third = [send_deep(tan3_wide, i, bottom) for i in range(3)]
+    lam_step(3)
 
     arrive(*border)
-    prefix_rows(1, slice(rows, ext_rows))
-    start_adjoint(1, mu)
-    pending = []
-    for n in range(4):
-        pending = mu_step(n, pending)
+    prefix_rows(1, bottom[0])
+    start_adjoint(1, mu, bottom[0])
+    arrive(*deep_third)
+    for n in range(3):
+        mu_step(n, [slice(rows - 8, ext_rows), slice(0, 8)])
+    mu_step(3, [slice(rows - 8, rows), slice(0, 8)])
     finish()
 
 
@@ -473,7 +499,7 @@
     def shards(states, direction, mixing, level_dz, lat_width, cost_weight, ocean_columns, atlantic, levels):
         layers, rows, columns = direction.shape
         ext = (rows + 2 * HALO, columns + 128)
-        tall = (layers + 1,) + ext
+        tall = (layers + DEEP,) + ext
         f32, i32 = jnp.float32, jnp.int32
         vmem = lambda *shape: pltpu.VMEM(shape, f32)
         dma = lambda count: pltpu.SemaphoreType.DMA((count,))
@@ -489,15 +515,15 @@
                 vmem(*states.shape), vmem(*direction.shape), vmem(*direction.shape),
                 pltpu.VMEM((rows, columns), i32), pltpu.VMEM((rows, columns), i32), pltpu.VMEM((rows, columns), i32),
                 vmem(*cost_weight.shape), pltpu.SMEM(level_dz.shape, f32), pltpu.SMEM(lat_width.shape, f32),
-                vmem(6, *tall), vmem(layers, *ext), vmem(*tall), vmem(*tall), vmem(*tall),
-                vmem(layers, *ext), vmem(4, *tall), vmem(4, *tall),
+                vmem(6, *tall), vmem(layers + 3, *ext), vmem(*tall), vmem(*tall), vmem(*tall),
+                vmem(*tall), vmem(4, *tall), vmem(4, *tall),
                 vmem(ext[0], 128 + ext[1]), vmem(layers, 2 * HALO, columns),
                 vmem(2, 3, layers // 2, 2 * HALO, columns), vmem(2, 3, layers // 2, 2 * HALO, columns),
                 vmem(2, 2, rows, 128), vmem(2, 2, ext[0], 128),
                 vmem(2, rows, 128), vmem(2, ext[0], 128), vmem(8, 128), vmem(8, 128),
                 vmem(2, 8, 128), vmem(2, 2 * n_lon, 8, 128), vmem(2, ext[0], 128),
-                vmem(2, layers + 1, ext[0], 128), vmem(n_depth * layers, ext[0], 128),
-                dma(9), dma(22), dma(22), dma(6), dma(6), dma(14), dma(14),
+                vmem(2, layers + DEEP, ext[0], 128), vmem(n_depth * layers, ext[0], 128),
+                dma(9), dma(22), dma(22), dma(6), dma(6), dma(28), dma(28),
                 pltpu.SemaphoreType.DMA((2, 2 * n_lon - 1)), pltpu.SemaphoreType.DMA((2, 2 * n_lon - 1)),
                 pltpu.SemaphoreType.REGULAR,
             ],

time: 38.7 us -> 36.9 us (0.953)
  Pallas kernels: 38 us -> 36.2 us
    pallas_call x1, Pallas kernels: 37.1 us -> 35.3 us  [shards(): pl.pallas_call(body, out_shape=(vmem(*direction.shape), vmem(*direction.s...]
where the time goes in v3:
time: 36.9 us; the launch traced here: 36.8 us
  Pallas kernels  36.2 us (98%)
  between operations  0.64 us (2%)
    pallas_call x1, Pallas kernels, shards(): pl.pallas_call(body, out_shape=(vmem(*direction.shape), vmem(*direction.s...  35.3 us
    pallas_call x1, Pallas kernels, shards(): pl.pallas_call(store, out_shape=tuple((jax.ShapeDtypeStruct(result.shape,...  0.86 us

profile of v3, /device:TPU:1, one launch (start us, length us, event | category | flops | bytes accessed | tf_op | source)
XLA Modules:
  0.0 36.8 jit_solution(14773622658005716930)
XLA Ops:
  0.6 35.3 %shard_map.112 = (f32[10,32,256]{2,1,0:T(8,128)S(1)}, f32[10,32,256]{2,1,0:T(8,128)S(1)}, f32[10,32]{1,0:T(8,128)S(1)}) custom-call(f32[4,10,32,256]{3,2,1,0:T(8,128)} %states.1, f32[10,32,256]{2,1,0:T(8,128)} %direction.1, f32[10,32,256]{2,1,0:T(8,128)} %mixing.1, f32[10]{0:T(128)} %dz_in_hbm.1, f32[32]{0:T(128)} %width_in_hbm.1, f32[20,32]{1,0:T(8,128)} %weight_in_hbm.1, ...), custom_call_target="tpu_custom_call" | custom-call | flops 30000000 | bytes 3000000 | tf_op jit(solution)/shard_map/pallas_call | solution.py:509
  35.9 0.9 %shard_map.113 = (f32[10,32,256]{2,1,0:T(8,128)}, f32[10,32,256]{2,1,0:T(8,128)}, f32[10,32]{1,0:T(8,128)}) custom-call(f32[10,32,256]{2,1,0:T(8,128)S(1)} %get-tuple-element.6.hess, f32[10,32,256]{2,1,0:T(8,128)S(1)} %get-tuple-element.7.grad, f32[10,32]{1,0:T(8,128)S(1)} %get-tuple-element.8.overturning), custom_call_target="tpu_custom_call" | custom-call | bytes 1000000 | tf_op jit(solution)/shard_map/pallas_call | solution.py:538

commit v4 on v3

--- a/solution.py
+++ b/solution.py
@@ -49,11 +49,14 @@
     def at(dl=0, dz=0, dd=0):
         return (wrap(lon + dl, n_lon), wrap(lat + dz, n_lat), wrap(dep + dd, n_depth))
 
-    plane = [(i, d) for d in range(n_depth) for i in range(n_lon) if i or d]
+    lines = n_lon // LINE
+    plane = [(i, k, d) for i in range(lines) for k in range(LINE) for d in range(n_depth) if i or k or d]
+    plane.sort(key=lambda offset: not (offset[0] and offset[1]))
     start = lon // LINE * LINE
-    across = [at(dl=LINE * i) for i in range(1, n_lon // LINE)]
+    in_line = lambda i: lax.rem(lon - start + i, LINE)
+    across = [at(dl=LINE * i) for i in range(1, lines)]
     peers = [
-        (start + lax.rem(lon - start + i, LINE), lat, wrap(dep + d, n_depth))
+        (start + in_line(i), lat, wrap(dep + d, n_depth))
         for d in range(n_depth) for i in range(LINE) if i or d
     ]
     peers += across + [at(dl=i) for i in (1, -1)] + [at(dz=z) for z in (1, -1)]
@@ -293,10 +296,12 @@
     def gather(f, sums):
         zone[f] = sums
         zones[f, lon] = sums
-        return [
-            send(zone.at[f], zones.at[f, lon + (n_lon if dd else 0)], zone_send.at[f, i], zone_recv.at[f, i], at(dl=dl, dd=dd))
-            for i, (dl, dd) in enumerate(plane)
-        ]
+        copies = []
+        for n, (i, k, d) in enumerate(plane):
+            device = (wrap(start + LINE * i, n_lon) + in_line(k), lat, wrap(dep + d, n_depth))
+            slot = lon + (n_lon if d else 0)
+            copies.append(send(zone.at[f], zones.at[f, slot], zone_send.at[f, n], zone_recv.at[f, n], device))
+        return copies
 
     last = drag[3]
     sums = jnp.zeros((8, 128), jnp.float32)
@@ -328,6 +333,7 @@
             capacity_at(j, part)
             tan1[(j,) + part] = tangent_at(0, j, part)
     pending = send_level(tan1)
+    deep = [send_deep(couple, i, whole) for i in (1, 2)]
 
     for s in (1, 2):
         nxt = tangents[s + 1]
@@ -337,23 +343,12 @@
                 arrive(pending)
             nxt[j] = tangent_at(s, j, whole)
         pending = send_level(nxt)
-
-    pair = [jnp.zeros((rows, 128), jnp.float32)] * 2
-    for j in range(layers):
-        block = tan3[(j,) + inner]
-        tan3_wide[(j,) + inner] = block
-        pack(pair, block, j)
-    strip3_out[0] = pair[0]
-    strip3_out[1] = pair[1]
-    strips = send_strips(strip3_out, strip3_in, 2)
-    third_rows = send_rows(tan3_wide, (every,), inner[1], 7)
-
-    sums = jnp.zeros((8, 128), jnp.float32)
-    for j in range(layers):
-        if j == bottom_level:
-            arrive(pending)
-        sums = put(sums, zonal(tangent_at(3, j, inner), j), j)
-    gathered_1 = gather(1, sums)
+        if s == 1:
+            deep += [send_deep(couple, 3, whole), send_deep(drag[1], 0, whole)]
+    arrive(*drag_rows[2])
+    deep += [send_deep(drag[3], 0, part) for part in frame]
+    deep += [send_deep(drag[t], i, whole) for t, i in ((3, 1), (3, 2), (2, 0), (2, 1))]
+    deep += [send_deep(tan2, 1, whole)]
 
     def collect(f):
         mine = zones[f, 0]
@@ -378,12 +373,35 @@
             prefixes[f, k, part] = prefix[k]
         return stream
 
-    arrive(*flat_rows, *drag_rows[2])
-    deep = [send_deep(couple, i, whole) for i in range(1, DEEP)]
-    deep += [send_deep(drag[3], 0, part) for part in frame]
-    deep += [send_deep(drag[s], i, whole) for s, i in ((3, 1), (3, 2), (2, 0), (2, 1), (1, 0))]
-    deep += [send_deep(tan2, 1, whole)]
+    sums = jnp.zeros((8, 128), jnp.float32)
+    for j in range(layers - 1):
+        sums = put(sums, zonal(tangent_at(3, j, inner), j), j)
+    pair = [jnp.zeros((rows, 128), jnp.float32)] * 2
+    for j in range(layers):
+        block = tan3[(j,) + inner]
+        tan3_wide[(j,) + inner] = block
+        pack(pair, block, j)
+    strip3_out[0] = pair[0]
+    strip3_out[1] = pair[1]
+    strips = send_strips(strip3_out, strip3_in, 2)
+    third_rows = send_rows(tan3_wide, (every,), inner[1], 7)
     deep_third = [send_deep(tan3_wide, i, inner) for i in range(3)]
+    for way, dl in ((0, 1), (1, -1)):
+        for n, (src, dst, dz) in enumerate((
+            (slice(0, HALO), slice(rows, rows + HALO), -1), (slice(rows - HALO, rows), slice(rows + HALO, ext_rows), 1)
+        )):
+            i = 4 + 2 * way + n
+            third_rows.append(send(
+                strip3_out.at[way, src], strip3_in.at[way, dst], lon_send.at[i + 2], lon_recv.at[i + 2], at(dl=dl, dz=dz)
+            ))
+
+    arrive(pending)
+    sums = put(sums, zonal(tangent_at(3, bottom_level, inner), bottom_level), bottom_level)
+    gathered_1 = gather(1, sums)
+    arrive(*gathered_0)
+    totals_0 = collect(0)
+
+    arrive(*flat_rows)
     for k in range(all_layers):
         weights[k] = jnp.broadcast_to(flat[:, k : k + 1], (ext_rows, 128))
 
@@ -399,12 +417,15 @@
         keep = capacity[at_part] - damp * damp
         return couple[at_part] * around(couple, ref.at[n], j, part) + keep * ref[(n,) + at_part], damp
 
-    def lam_step(n):
+    def lam_step(n, bands):
         for j in range(layers + 3 - n):
-            if n < 3:
-                lam[n + 1, j] = adjoint_at(lam, n, j, whole)[0]
-            else:
-                grad[own(j)] = adjoint_at(lam, n, j, inner)[0]
+            for band in bands:
+                part = (band, whole[1] if n < 3 else inner[1])
+                new = adjoint_at(lam, n, j, part)[0]
+                if n < 3:
+                    lam[(n + 1, j) + part] = new
+                else:
+                    grad[(own(j),) + part] = new
 
     ratio = 6.0 * cubic_drag / math.sqrt(3.0 * cubic_drag)
 
@@ -420,52 +441,47 @@
                 else:
                     hess[(own(j),) + part] = new
 
-    arrive(*gathered_0)
-    border = collect(0)
     streams = prefix_rows(0, inner[0])
     spots = lax.broadcasted_iota(jnp.int32, (rows, rows), 0) == lax.broadcasted_iota(jnp.int32, (rows, rows), 1)
     for j in range(layers):
         line = jnp.sum(jnp.where(spots, streams[j][:, 0:rows], 0.0), axis=0, keepdims=True)
         overturning[pl.ds(own(j), 1), :] = line
-    arrive(*strips)
-    corners = send_rows(strip3_in, (slice(0, 2),), slice(0, 128), 10)
-    both = combine(strip3_in, inner[0])
-    for j in range(layers):
-        tan3_wide[(j,) + side] = unpack(both, j)
-    deep_third += [send_deep(tan3_wide, i, side) for i in range(3)]
     arrive(*deep)
     for j in range(layers, layers + 3):
         capacity_at(j, whole)
     start_adjoint(0, lam, inner[0])
-    arrive(*border)
-    prefix_rows(0, bottom[0])
-    start_adjoint(0, lam, bottom[0])
-    lam_step(0)
-    lam_step(1)
+    for n in range(3):
+        lam_step(n, [inner[0]])
+    lam_step(3, [slice(8, rows - 8)])
+    arrive(*strips)
+    both = combine(strip3_in, inner[0])
+    for j in range(layers):
+        tan3_wide[(j,) + side] = unpack(both, j)
+    deep_third += [send_deep(tan3_wide, i, side) for i in range(3)]
 
     arrive(*gathered_1)
     border = collect(1)
     prefix_rows(1, inner[0])
     start_adjoint(1, mu, inner[0])
-    arrive(*deep_third)
-    lam_step(2)
-    for n in range(3):
-        mu_step(n, [inner[0]])
-    mu_step(3, [slice(8, rows - 8)])
-    arrive(*third_rows, *corners)
+    arrive(*deep_third, *third_rows)
     both = combine(strip3_in, bottom[0])
     for j in range(layers):
         tan3_wide[j, bottom[0], columns:] = unpack(both, j)
     deep_third = [send_deep(tan3_wide, i, bottom) for i in range(3)]
-    lam_step(3)
+    arrive(*totals_0)
+    prefix_rows(0, bottom[0])
+    start_adjoint(0, lam, bottom[0])
+    for n in range(3):
+        lam_step(n, [slice(rows - 8, ext_rows), slice(0, 8)])
+    lam_step(3, [slice(rows - 8, rows), slice(0, 8)])
 
     arrive(*border)
     prefix_rows(1, bottom[0])
     start_adjoint(1, mu, bottom[0])
     arrive(*deep_third)
     for n in range(3):
-        mu_step(n, [slice(rows - 8, ext_rows), slice(0, 8)])
-    mu_step(3, [slice(rows - 8, rows), slice(0, 8)])
+        mu_step(n, [whole[0]])
+    mu_step(3, [inner[0]])
     finish()
 
 
@@ -523,7 +539,7 @@
                 vmem(2, rows, 128), vmem(2, ext[0], 128), vmem(8, 128), vmem(8, 128),
                 vmem(2, 8, 128), vmem(2, 2 * n_lon, 8, 128), vmem(2, ext[0], 128),
                 vmem(2, layers + DEEP, ext[0], 128), vmem(n_depth * layers, ext[0], 128),
-                dma(9), dma(22), dma(22), dma(6), dma(6), dma(28), dma(28),
+                dma(9), dma(20), dma(20), dma(10), dma(10), dma(28), dma(28),
                 pltpu.SemaphoreType.DMA((2, 2 * n_lon - 1)), pltpu.SemaphoreType.DMA((2, 2 * n_lon - 1)),
                 pltpu.SemaphoreType.REGULAR,
             ],

time: 36.9 us -> 36 us (0.976)
  Pallas kernels: 36.2 us -> 35.2 us
    pallas_call x1, Pallas kernels: 35.3 us -> 34.4 us  [shards(): pl.pallas_call(body, out_shape=(vmem(*direction.shape), vmem(*direction.s...]
where the time goes in v4:
time: 36 us; the launch traced here: 35.9 us
  Pallas kernels  35.2 us (98%)
  between operations  0.64 us (2%)
    pallas_call x1, Pallas kernels, shards(): pl.pallas_call(body, out_shape=(vmem(*direction.shape), vmem(*direction.s...  34.4 us
    pallas_call x1, Pallas kernels, shards(): pl.pallas_call(store, out_shape=tuple((jax.ShapeDtypeStruct(result.shape,...  0.86 us

profile of v4, /device:TPU:1, one launch (start us, length us, event | category | flops | bytes accessed | tf_op | source)
XLA Modules:
  0.0 35.9 jit_solution(14707561392474431537)
XLA Ops:
  0.6 34.4 %shard_map.112 = (f32[10,32,256]{2,1,0:T(8,128)S(1)}, f32[10,32,256]{2,1,0:T(8,128)S(1)}, f32[10,32]{1,0:T(8,128)S(1)}) custom-call(f32[4,10,32,256]{3,2,1,0:T(8,128)} %states.1, f32[10,32,256]{2,1,0:T(8,128)} %direction.1, f32[10,32,256]{2,1,0:T(8,128)} %mixing.1, f32[10]{0:T(128)} %dz_in_hbm.1, f32[32]{0:T(128)} %width_in_hbm.1, f32[20,32]{1,0:T(8,128)} %weight_in_hbm.1, ...), custom_call_target="tpu_custom_call" | custom-call | flops 30000000 | bytes 3000000 | tf_op jit(solution)/shard_map/pallas_call | solution.py:525
  35.0 0.9 %shard_map.113 = (f32[10,32,256]{2,1,0:T(8,128)}, f32[10,32,256]{2,1,0:T(8,128)}, f32[10,32]{1,0:T(8,128)}) custom-call(f32[10,32,256]{2,1,0:T(8,128)S(1)} %get-tuple-element.6.hess, f32[10,32,256]{2,1,0:T(8,128)S(1)} %get-tuple-element.7.grad, f32[10,32]{1,0:T(8,128)S(1)} %get-tuple-element.8.overturning), custom_call_target="tpu_custom_call" | custom-call | bytes 1000000 | tf_op jit(solution)/shard_map/pallas_call | solution.py:554
